TPU v7x, 32 devices: a whole 2x2x4 slice. The times are simulated.
32 devices in a mesh: pass: 4 (over x, core), dp: 8 (over z, y).
Axes of the slice: x: 2, y: 2, z: 4, core: 2. Of those that a mesh axis runs over, the one named last changes fastest.
Arguments:
- block_input: bfloat16 [4, 6144, 768], P('pass', 'dp'), may hold values from -6 to 6
- segments: int32 [6144], P('dp'), may hold values from 0 to 23, as said below
- pass_emb: float32 [4, 768], replicated, may hold values from -3 to 3
- gain_attn: float32 [768], replicated, may hold values from 0.1 to 1.9
- w_qkv: bfloat16 [768, 2304], replicated, may hold values from -0.21875 to 0.21875
- w_out: bfloat16 [768, 768], replicated, may hold values from -1.25 to 1.25
- gain_mlp: float32 [768], replicated, may hold values from 0.1 to 1.9
- w_up: bfloat16 [768, 3072], replicated, may hold values from -0.21875 to 0.21875
- w_down: bfloat16 [3072, 768], replicated, may hold values from -0.109375 to 0.109375
- cotangent: bfloat16 [4, 6144, 768], P('pass', 'dp'), may hold values from -6 to 6
Outputs:
- block_output: bfloat16 [4, 6144, 768], P('pass', 'dp')
- grad_input: bfloat16 [4, 6144, 768], P('pass', 'dp')
- grad_pass_emb: float32 [4, 768], replicated
- grad_gain_attn: float32 [768], replicated
- grad_w_qkv: float32 [768, 2304], replicated
- grad_w_out: float32 [768, 768], replicated
- grad_gain_mlp: float32 [768], replicated
- grad_w_up: float32 [768, 3072], replicated
- grad_w_down: float32 [3072, 768], replicated
Inputs may be any that keep to these rules, and one draw needn't show every extreme that they name: `segments`: within each aligned block of 768 positions (one index of dp) the ids never fall and the block holds either one sequence of 768 positions or 3 sequences of 256 positions; different blocks have different ids. The first block holds short sequences and the second one long sequence.
All inputs are finite; a program needn't handle non-finite values.
Results may differ from a plain program's by a relative error of at most 0.015.
Values may be sent and summed in bfloat16 or wider, within the bound.
No kernel may reach another device: no remote copies, remote signals or barrier semaphores. Data moves between devices by JAX's collectives and lax.ppermute only.
A program may use at most 192 MiB of HBM per device.

v0:
```python
import jax
import jax.numpy as jnp
from jax import lax
from jax.sharding import PartitionSpec as P

D = 768
HEADS = 12
HEAD_DIM = 64
SHORT = 256


def layer_norm(hidden, gain_vec):
    center = hidden - jnp.mean(hidden, axis=-1, keepdims=True)
    spread = jnp.mean(center * center, axis=-1, keepdims=True)
    return center * lax.rsqrt(spread + 1e-05) * gain_vec


def gelu_tanh(values):
    return jax.nn.gelu(values, approximate=True)


def contract_rows(left_mat, right_mat):
    return lax.dot_general(
        left_mat, right_mat, (((0,), (0,)), ((), ())), preferred_element_type=jnp.float32
    )


def times_transpose(left_mat, right_mat):
    return lax.dot_general(
        left_mat, right_mat, (((1,), (1,)), ((), ())), preferred_element_type=jnp.float32
    )


def block_scores(queries, keys_all, seg_local, block_idx, pass_here):
    length = queries.shape[0]
    first_row = block_idx * SHORT
    key_rows = lax.dynamic_slice_in_dim(keys_all, first_row, SHORT, 0).reshape(
        SHORT, HEADS, HEAD_DIM
    )
    scores = jnp.einsum(
        "qhd,khd->hqk", queries, key_rows, preferred_element_type=jnp.float32
    ) * HEAD_DIM ** (-0.5)
    key_first = first_row % length
    key_pos = key_first + jnp.arange(SHORT)
    key_seg = lax.dynamic_slice_in_dim(seg_local, key_first, SHORT, 0)
    query_pos = jnp.arange(length)
    allowed = (
        (key_pos[None, :] <= query_pos[:, None])
        & (key_seg[None, :] == seg_local[:, None])
        & (first_row // length <= pass_here)
    )
    return (jnp.where(allowed[None], scores, -1e30), key_rows)


def value_block(values_all, block_idx):
    return lax.dynamic_slice_in_dim(values_all, block_idx * SHORT, SHORT, 0).reshape(
        SHORT, HEADS, HEAD_DIM
    )


def attention_forward(queries, keys_all, values_all, seg_local, pass_here):
    length = queries.shape[0]
    block_count = (pass_here + 1) * (length // SHORT)

    def online_step(block_idx, running):
        row_max, row_sum, accum = running
        masked, key_rows = block_scores(queries, keys_all, seg_local, block_idx, pass_here)
        new_max = jnp.maximum(row_max, jnp.max(masked, axis=-1))
        factor = jnp.exp(row_max - new_max)
        raw = jnp.exp(masked - new_max[..., None])
        row_sum = row_sum * factor + jnp.sum(raw, axis=-1)
        accum = accum * factor.T[..., None] + jnp.einsum(
            "hqk,khd->qhd",
            raw.astype(jnp.bfloat16),
            value_block(values_all, block_idx),
            preferred_element_type=jnp.float32,
        )
        return (new_max, row_sum, accum)

    start_max = jnp.full((HEADS, length), -1e30, jnp.float32)
    start = (
        start_max,
        jnp.zeros((HEADS, length), jnp.float32),
        jnp.zeros((length, HEADS, HEAD_DIM), jnp.float32),
    )
    row_max, row_sum, accum = lax.fori_loop(0, block_count, online_step, start)
    log_total = row_max + jnp.log(row_sum)
    attended_f32 = accum / row_sum.T[..., None]
    return (attended_f32.reshape(length, D).astype(jnp.bfloat16), attended_f32, log_total)


def attention_backward(
    queries, keys_all, values_all, seg_local, pass_here, log_total, attended_f32, grad_attended
):
    length = queries.shape[0]
    grad_heads = grad_attended.reshape(length, HEADS, HEAD_DIM)
    score_scale = HEAD_DIM ** (-0.5)
    row_delta = jnp.einsum("qhd,qhd->hq", grad_heads.astype(jnp.float32), attended_f32)
    total_blocks = keys_all.shape[0] // SHORT

    def sweep_step(grad_queries, block_idx):

        def active(carry):
            masked, key_rows = block_scores(queries, keys_all, seg_local, block_idx, pass_here)
            weights = jnp.exp(masked - log_total[..., None])
            value_rows = value_block(values_all, block_idx)
            grad_probs = jnp.einsum(
                "qhd,khd->hqk", grad_heads, value_rows, preferred_element_type=jnp.float32
            )
            grad_scores = (weights * (grad_probs - row_delta[..., None])).astype(jnp.bfloat16)
            prob_bf = weights.astype(jnp.bfloat16)
            carry = carry + jnp.einsum(
                "hqk,khd->qhd", grad_scores, key_rows, preferred_element_type=jnp.float32
            )
            grad_keys = (
                jnp.einsum("hqk,qhd->khd", grad_scores, queries, preferred_element_type=jnp.float32)
                * score_scale
            )
            grad_values = jnp.einsum(
                "hqk,qhd->khd", prob_bf, grad_heads, preferred_element_type=jnp.float32
            )
            piece = jnp.concatenate(
                [grad_keys.reshape(SHORT, D), grad_values.reshape(SHORT, D)], axis=1
            )
            return (carry, piece)

        def empty(carry):
            return (carry, jnp.zeros((SHORT, 2 * D), jnp.float32))

        return lax.cond(block_idx * SHORT // length <= pass_here, active, empty, grad_queries)

    start = jnp.zeros((length, HEADS, HEAD_DIM), jnp.float32)
    grad_queries, pieces = lax.scan(sweep_step, start, jnp.arange(total_blocks))
    grad_queries = (grad_queries * score_scale).reshape(length, D).astype(jnp.bfloat16)
    kv_terms = pieces.reshape(total_blocks * SHORT, 2 * D)
    grad_kv = lax.psum_scatter(
        kv_terms.astype(jnp.bfloat16), "pass", scatter_dimension=0, tiled=True
    )
    return (grad_queries, grad_kv)


def on_device(
    block_input, segments, pass_emb, gain_attn, w_qkv, w_out, gain_mlp, w_up, w_down, cotangent
):
    pass_here = lax.axis_index("pass")
    passes = pass_emb.shape[0]
    emb_row = lax.dynamic_index_in_dim(pass_emb, pass_here, 0, keepdims=False)
    hidden = block_input[0].astype(jnp.float32) + emb_row
    normed_val, norm_attn_pull = jax.vjp(layer_norm, hidden, gain_attn)
    normed = normed_val.astype(jnp.bfloat16)
    projected = jnp.dot(normed, w_qkv, preferred_element_type=jnp.float32).astype(jnp.bfloat16)
    queries_flat = projected[:, :D]
    keys_all, values_all = (
        lax.all_gather(projected[:, D : 2 * D], "pass", axis=0, tiled=True),
        lax.all_gather(projected[:, 2 * D :], "pass", axis=0, tiled=True),
    )
    length = queries_flat.shape[0]
    queries = queries_flat.reshape(length, HEADS, HEAD_DIM)
    attended, attended_f32, log_total = attention_forward(
        queries, keys_all, values_all, segments, pass_here
    )
    residual = hidden + jnp.dot(attended, w_out, preferred_element_type=jnp.float32)
    normed2_val, norm_mlp_pull = jax.vjp(layer_norm, residual, gain_mlp)
    normed2 = normed2_val.astype(jnp.bfloat16)
    up_proj = jnp.dot(normed2, w_up, preferred_element_type=jnp.float32)
    activated_val, gelu_pull = jax.vjp(gelu_tanh, up_proj)
    activated = activated_val.astype(jnp.bfloat16)
    output = (residual + jnp.dot(activated, w_down, preferred_element_type=jnp.float32)).astype(
        jnp.bfloat16
    )
    grad_out = cotangent[0]
    grad_w_down = contract_rows(activated, grad_out)
    grad_act = times_transpose(grad_out, w_down)
    grad_up = gelu_pull(grad_act)[0].astype(jnp.bfloat16)
    grad_w_up = contract_rows(normed2, grad_up)
    grad_normed2 = times_transpose(grad_up, w_up)
    grad_resid_norm, grad_gain_mlp = norm_mlp_pull(grad_normed2)
    grad_residual = grad_out.astype(jnp.float32) + grad_resid_norm
    grad_attn = grad_residual.astype(jnp.bfloat16)
    grad_w_out = contract_rows(attended, grad_attn)
    grad_attended = times_transpose(grad_attn, w_out).astype(jnp.bfloat16)
    grad_queries, grad_kv = attention_backward(
        queries, keys_all, values_all, segments, pass_here, log_total, attended_f32, grad_attended
    )
    grad_w_query = contract_rows(normed, grad_queries)
    grad_w_keyval = contract_rows(normed, grad_kv)
    grad_normed = times_transpose(grad_queries, w_qkv[:, :D]) + times_transpose(
        grad_kv, w_qkv[:, D:]
    )
    grad_hidden_norm, grad_gain_attn = norm_attn_pull(grad_normed)
    grad_hidden = grad_residual + grad_hidden_norm
    selector = (jnp.arange(passes) == pass_here).astype(jnp.float32)
    grad_emb_cols = jnp.sum(grad_hidden, axis=0)[:, None] * selector[None, :]
    small_grads = jnp.concatenate(
        [grad_emb_cols, grad_gain_attn[:, None], grad_gain_mlp[:, None]], axis=1
    )
    share_q, share_kv, share_out, share_up, share_down, share_small = (
        lax.psum_scatter(grad_w_query, "dp", scatter_dimension=0, tiled=True),
        lax.psum_scatter(grad_w_keyval, "dp", scatter_dimension=0, tiled=True),
        lax.psum_scatter(grad_w_out, "dp", scatter_dimension=0, tiled=True),
        lax.psum_scatter(grad_w_up, "dp", scatter_dimension=0, tiled=True),
        lax.psum_scatter(grad_w_down, "dp", scatter_dimension=0, tiled=True),
        lax.psum_scatter(small_grads, "dp", scatter_dimension=0, tiled=True),
    )
    share_q, share_kv, share_out, share_up, share_down, share_small = (
        lax.psum(share_q.astype(jnp.bfloat16), "pass").astype(jnp.float32),
        lax.psum(share_kv.astype(jnp.bfloat16), "pass").astype(jnp.float32),
        lax.psum(share_out.astype(jnp.bfloat16), "pass").astype(jnp.float32),
        lax.psum(share_up.astype(jnp.bfloat16), "pass").astype(jnp.float32),
        lax.psum(share_down.astype(jnp.bfloat16), "pass").astype(jnp.float32),
        lax.psum(share_small.astype(jnp.bfloat16), "pass").astype(jnp.float32),
    )
    total_q, total_kv, out_total, up_total, down_total, small_total = (
        lax.all_gather(share_q.astype(jnp.bfloat16), "dp", axis=0, tiled=True).astype(
            share_q.dtype
        ),
        lax.all_gather(share_kv.astype(jnp.bfloat16), "dp", axis=0, tiled=True).astype(
            share_kv.dtype
        ),
        lax.all_gather(share_out.astype(jnp.bfloat16), "dp", axis=0, tiled=True).astype(
            share_out.dtype
        ),
        lax.all_gather(share_up.astype(jnp.bfloat16), "dp", axis=0, tiled=True).astype(
            share_up.dtype
        ),
        lax.all_gather(share_down.astype(jnp.bfloat16), "dp", axis=0, tiled=True).astype(
            share_down.dtype
        ),
        lax.all_gather(share_small.astype(jnp.bfloat16), "dp", axis=0, tiled=True).astype(
            share_small.dtype
        ),
    )
    qkv_total = jnp.concatenate([total_q, total_kv], axis=1)
    emb_total = small_total[:, :passes].T
    gain_attn_total = small_total[:, passes]
    gain_mlp_total = small_total[:, passes + 1]
    return (
        output[None],
        grad_hidden.astype(jnp.bfloat16)[None],
        emb_total,
        gain_attn_total,
        qkv_total,
        out_total,
        gain_mlp_total,
        up_total,
        down_total,
    )


def solution(mesh):
    in_specs = (
        P("pass", "dp", None),
        P("dp"),
        P(),
        P(),
        P(),
        P(),
        P(),
        P(),
        P(),
        P("pass", "dp", None),
    )
    out_specs = (P("pass", "dp", None), P("pass", "dp", None), P(), P(), P(), P(), P(), P(), P())
    return jax.shard_map(
        on_device, mesh=mesh, in_specs=in_specs, out_specs=out_specs, check_vma=False
    )
```

profile of v0, /device:TPU:0, one launch (start us, length us, event | category | flops | bytes accessed | tf_op | source)
XLA Modules:
  0.0 1559.4 jit_solution(17017527128239423490)
XLA Ops:
  11.7 5.5 convolution_convert_fusion
  23.0 36.1 %all-gather.11.cloned.1.call-done = bf16[3072,768]{1,0:T(8,128)(2,1)} async-done(((bf16[768,768]{1,0:T(8,128)(2,1)}), bf16[3072,768]{1,0:T(8,128)(2,1)}) %all-gather.11.cloned.1.call-update) | async-done | bytes 4718608 | tf_op jit(solution)/shard_map/all_gather | solution.py:155
  59.1 6.6 copy.104
  65.8 33.0 %all-gather.9.cloned.1.call-done = bf16[3072,768]{1,0:T(8,128)(2,1)} async-done(((bf16[768,768]{1,0:T(8,128)(2,1)}), bf16[3072,768]{1,0:T(8,128)(2,1)}) %all-gather.9.cloned.1.call-update) | async-done | bytes 4718608 | tf_op jit(solution)/shard_map/all_gather | solution.py:154
  98.8 6.6 copy.103
  106.9 26.0 %while.33 = (s32[]{:T(128)}, f32[12,768]{1,0:T(8,128)}, f32[12,768]{1,0:T(8,128)}, f32[768,12,64]{0,2,1:T(8,128)S(1)}, s32[]{:T(128)}, /*index=5*/s32[768]{0:T(1...) while((s32[]{:T(128)}, f32[12,768]{1,0:T(8,128)}, ...), condition=%wide.region_5.6_spmd, body=%wide.region_2.5_spmd.sunk | while | flops 631926016 | bytes 43114972 | solution.py:86
  112.1 2.8 bitcast_add_fusion.3
  120.8 2.8 bitcast_add_fusion.3
  129.4 2.8 bitcast_add_fusion.3
  139.1 4.0 fusion.76
  143.2 10.4 fusion.33
  153.6 7.1 multiply_reduce_fusion
  165.9 124.7 %while.34 = (s32[]{:T(128)}, f32[768,12,64]{0,2,1:T(8,128)S(1)}, bf16[12,256,1536]{2,1,0:T(8,128)(2,1)}, s32[12]{0:T(128)}, s32[]{:T(128)}, /*index=5*/bf16[3072...) while((s32[]{:T(128)}, f32[768,12,64]{0,2,1:T(8,128)S(1)}, ...), condition=%wide.region_13.14_spmd, body=%wide.region_10.13_spmd.sunk | while | flops 1536884992 | bytes 65884840 | solution.py:133
  168.1 13.0 conditional.2
  171.9 2.2 fusion.20
  174.1 3.4 fusion.16
  181.1 2.3 copy.149
  187.5 13.0 conditional.2
  191.3 2.3 fusion.20
  193.6 3.4 fusion.16
  200.5 2.3 copy.149
  206.9 13.0 conditional.2
  210.7 2.3 fusion.20
  213.0 3.4 fusion.16
  219.9 2.3 copy.149
  227.3 2.3 copy.149
  234.7 2.3 copy.149
  242.0 2.3 copy.149
  249.4 2.3 copy.149
  256.7 2.3 copy.149
  264.1 2.3 copy.149
  271.5 2.3 copy.149
  278.8 2.3 copy.149
  286.2 2.3 copy.149
  291.8 3.8 fusion.85
  297.0 2.7 fusion.58
  300.9 12.7 fusion.60
  315.3 8.8 fusion.75
  324.1 231.3 %reduce-scatter.10.cloned.1.call-done = bf16[768,1536]{1,0:T(8,128)(2,1)} async-done(((bf16[3072,1536]{1,0:T(8,128)(2,1)}), bf16[768,1536]{1,0:T(8,128)(2,1)}) %reduce-scatter.10.cloned.1.call-update) | async-done | bytes 2359312 | tf_op jit(solution)/shard_map/reduce_scatter | solution.py:136
  555.5 6.0 fusion.77
  563.4 64.6 %reduce-scatter.16.cloned.1.call-done = f32[96,768]{1,0:T(8,128)} async-done(((f32[768,768]{1,0:T(8,128)}), f32[96,768]{1,0:T(8,128)}) %reduce-scatter.16.cloned.1.call-update) | async-done | bytes 294928 | tf_op jit(solution)/shard_map/reduce_scatter | solution.py:200
  629.6 70.0 %reduce-scatter.12.cloned.1.call-done = f32[96,768]{1,0:T(8,128)} async-done(((f32[768,768]{1,0:T(8,128)}), f32[96,768]{1,0:T(8,128)}) %reduce-scatter.12.cloned.1.call-update) | async-done | bytes 294928 | tf_op jit(solution)/shard_map/reduce_scatter | solution.py:198
  701.2 164.3 %reduce-scatter.20.cloned.1.call-done = f32[384,768]{1,0:T(8,128)} async-done(((f32[3072,768]{1,0:T(8,128)}), f32[384,768]{1,0:T(8,128)}) %reduce-scatter.20.cloned.1.call-update) | async-done | bytes 1179664 | tf_op jit(solution)/shard_map/reduce_scatter | solution.py:202
  867.7 164.0 %reduce-scatter.18.cloned.1.call-done = f32[96,3072]{1,0:T(8,128)} async-done(((f32[768,3072]{1,0:T(8,128)}), f32[96,3072]{1,0:T(8,128)}) %reduce-scatter.18.cloned.1.call-update) | async-done | bytes 1179664 | tf_op jit(solution)/shard_map/reduce_scatter | solution.py:201
  1031.8 2.2 convert_element_type.161
  1033.9 4.5 fusion.53
  1038.4 2.6 fusion.47
  1043.9 86.7 %reduce-scatter.14.cloned.1.call-done = f32[96,1536]{1,0:T(8,128)} async-done(((f32[768,1536]{1,0:T(8,128)}), f32[96,1536]{1,0:T(8,128)}) %reduce-scatter.14.cloned.1.call-update) | async-done | bytes 589840 | tf_op jit(solution)/shard_map/reduce_scatter | solution.py:199
  1133.3 4.6 fusion.72
  1139.0 41.4 %all-reduce.3.cloned.1.call-done = (bf16[96,1536]{1,0:T(8,128)(2,1)}, bf16[96,768]{1,0:T(8,128)(2,1)}, bf16[96,768]{1,0:T(8,128)(2,1)}, bf16[96,3072]{1,0:T(8,128)(2,1)}, bf16[384,768]{1,0:T(8,128)(2,1)}) async-done(((bf16[96,1536]{1,0:T(8,128)(2,1)}, bf16[96,768]{1,0:T(8,128)(2,1)}, bf16[96,768]{1,0:T(8,128)(2,1)}, bf16[96,3072]{1,0:T(8,128)(2,1)}, bf16[384,768]{1,0:T(8,128)(2,1)}), ...) | async-done | bytes 1769488 | tf_op jit(solution)/shard_map/psum | solution.py:207
  1183.0 10.4 fusion.56
  1193.4 2.5 copy.115
  1197.3 48.8 %reduce-scatter.22.cloned.1.call-done = f32[96,6]{1,0:T(8,128)} async-done(((f32[768,6]{1,0:T(8,128)}), f32[96,6]{1,0:T(8,128)}) %reduce-scatter.22.cloned.1.call-update) | async-done | bytes 2320
  1247.0 5.7 psum.42
  1252.6 26.1 %all-gather = bf16[8,96,6]{1,2,0:T(8,128)(2,1)S(1)} all-gather(bf16[1,96,6]{1,2,0:T(8,128)(2,1)S(1)} %bitcast.193), channel_id=1, replica_groups=mesh['pass'=4,'dp'=8] {'dp'}, dimensions={0}, use_global_device_ids=true | all-gather | bytes 10368 | tf_op jit(solution)/shard_map/all_gather | solution.py:229
  1280.1 8.6 all-gather.17.cloned.1.call-done
  1288.7 2.8 convert_element_type.160
  1291.5 39.3 %all-gather.13.cloned.1.call-done = bf16[768,768]{1,0:T(8,128)(2,1)} async-done(((bf16[96,768]{1,0:T(8,128)(2,1)}), bf16[768,768]{1,0:T(8,128)(2,1)}) %all-gather.13.cloned.1.call-update) | async-done | bytes 1179664 | tf_op jit(solution)/shard_map/all_gather | solution.py:214
  1330.8 53.3 %all-gather.15.cloned.1.call-done = bf16[768,1536]{1,0:T(8,128)(2,1)} async-done(((bf16[96,1536]{1,0:T(8,128)(2,1)}), bf16[768,1536]{1,0:T(8,128)(2,1)}) %all-gather.15.cloned.1.call-update) | async-done | bytes 2359312 | tf_op jit(solution)/shard_map/all_gather | solution.py:217
  1384.1 5.5 maximum_convert_fusion
  1389.6 75.3 %all-gather.21.cloned.1.call-done = bf16[3072,768]{1,0:T(8,128)(2,1)} async-done(((bf16[384,768]{1,0:T(8,128)(2,1)}), bf16[3072,768]{1,0:T(8,128)(2,1)}) %all-gather.21.cloned.1.call-update) | async-done | bytes 4718608 | tf_op jit(solution)/shard_map/all_gather | solution.py:226
  1464.8 6.8 convert_element_type.164
  1471.6 73.5 %all-gather.19.cloned.1.call-done = bf16[768,3072]{1,0:T(8,128)(2,1)} async-done(((bf16[96,3072]{1,0:T(8,128)(2,1)}), bf16[768,3072]{1,0:T(8,128)(2,1)}) %all-gather.19.cloned.1.call-update) | async-done | bytes 4718608 | tf_op jit(solution)/shard_map/all_gather | solution.py:223
  1545.1 7.5 convert_element_type.162
  (306 shorter events, 143.3 us)
Async XLA Ops:
  7.2 128.3 %copy-start = (bf16[768,768]{1,0:T(8,128)(2,1)S(1)}, bf16[768,768]{1,0:T(8,128)(2,1)}, u32[]{:S(2)}) copy-start(bf16[768,768]{1,0:T(8,128)(2,1)} %param.21) | copy-start | bytes 3538948
  7.2 52.0 %all-gather.11.cloned.1.call-start = ((), (), s32[]{:S(2)}) async-start(), calls=%async_computation.8 | async-start | bytes 5898240 | tf_op jit(solution)/shard_map/all_gather | solution.py:155
  7.2 4.5 copy-start.43
  8.9 8.2 copy-start.4
  9.7 125.8 %copy-start.30 = (f32[768]{0:T(1024)}, f32[768]{0:T(1024)S(1)}, u32[]{:S(2)}) copy-start(f32[768]{0:T(1024)S(1)} %dynamic-slice_reduce_fusion) | copy-start | bytes 9220
  18.8 79.9 %all-gather.9.cloned.1.call-start = ((), (), s32[]{:S(2)}) async-start(), calls=%async_computation.7 | async-start | bytes 5898240 | tf_op jit(solution)/shard_map/all_gather | solution.py:154
  19.6 535.9 %reduce-scatter.10.cloned.1.call-start = ((), (), s32[]{:S(2)}) async-start(), calls=%async_computation.9 | async-start | bytes 11796480 | tf_op jit(solution)/shard_map/reduce_scatter | solution.py:136
  105.4 1.5 copy-start.28
  106.9 1.5 copy-start.2
  108.5 1.7 copy-start.13
  112.1 2.8 copy-start.15
  115.6 1.5 copy-start.2
  117.1 1.7 copy-start.13
  120.8 2.8 copy-start.15
  124.2 1.5 copy-start.2
  125.8 1.7 copy-start.13
  129.4 2.8 copy-start.15
  132.9 2.6 copy-start.5
  135.5 3.5 slice-start
  135.5 3.5 slice-start.1
  135.5 7.6 slice-start.2
  136.8 23.9 %copy-start.7 = (f32[768,768]{0,1:T(8,128)}, f32[768,768]{0,1:T(8,128)S(1)}, u32[]{:S(2)}) copy-start(f32[768,768]{0,1:T(8,128)S(1)} %get-tuple-element.561) | copy-start | bytes 7077892
  136.8 2.3 copy-start.29
  139.1 4.0 copy-start.25
  139.1 4.0 slice-start.3
  143.2 10.5 copy-start.11
  161.3 1.5 copy-start.9
  161.4 1.5 copy-start.40
  163.9 1.9 copy-start.20
  164.0 1.9 copy-start.3
  170.4 1.5 copy-start.21
  170.4 1.5 copy-start.36
  171.9 2.3 copy-start.35
  189.8 1.5 copy-start.21
  189.8 1.5 copy-start.36
  191.3 2.3 copy-start.35
  209.2 1.5 copy-start.21
  209.2 1.5 copy-start.36
  210.7 2.3 copy-start.35
  290.6 337.4 %reduce-scatter.16.cloned.1.call-start = ((), (), s32[]{:S(2)}) async-start(), calls=%async_computation.14 | async-start | bytes 2654208 | tf_op jit(solution)/shard_map/reduce_scatter | solution.py:200
  295.7 1.3 copy-start.6
  295.7 403.9 %reduce-scatter.12.cloned.1.call-start = ((), (), s32[]{:S(2)}) async-start(), calls=%async_computation.10 | async-start | bytes 2654208 | tf_op jit(solution)/shard_map/reduce_scatter | solution.py:198
  299.7 565.9 %reduce-scatter.20.cloned.1.call-start = ((), (), s32[]{:S(2)}) async-start(), calls=%async_computation.18 | async-start | bytes 10616832 | tf_op jit(solution)/shard_map/reduce_scatter | solution.py:202
  313.6 1.7 copy-start.8
  313.7 718.1 %reduce-scatter.18.cloned.1.call-start = ((), (), s32[]{:S(2)}) async-start(), calls=%async_computation.16 | async-start | bytes 10616832 | tf_op jit(solution)/shard_map/reduce_scatter | solution.py:201
  324.1 231.4 %copy-start.34 = (f32[768]{0:T(1024)S(1)}, f32[768]{0:T(1024)}, u32[]{:S(2)}) copy-start(f32[768]{0:T(1024)} %copy-done.32) | copy-start | bytes 9220
  324.1 231.4 %copy-start.39 = (f32[768]{0:T(1024)S(1)}, f32[768]{0:T(1024)}, u32[]{:S(2)}) copy-start(f32[768]{0:T(1024)} %copy-done.37) | copy-start | bytes 9220
  324.1 231.4 %copy-start.45 = (f32[768]{0:T(1024)S(1)}, f32[768]{0:T(1024)}, u32[]{:S(2)}) copy-start(f32[768]{0:T(1024)} %param.19) | copy-start | bytes 9220
  324.1 806.4 %reduce-scatter.14.cloned.1.call-start = ((), (), s32[]{:S(2)}) async-start(), calls=%async_computation.12 | async-start | bytes 5308416 | tf_op jit(solution)/shard_map/reduce_scatter | solution.py:199
  561.5 619.0 %all-reduce.3.cloned.1.call-start = ((), (), s32[]{:S(2)}) async-start(), calls=%async_computation.21 | async-start | bytes 3538944 | tf_op jit(solution)/shard_map/psum | solution.py:207
  1033.9 4.5 copy-start.23
  1038.4 2.7 copy-start.42
  1038.4 4.0 copy-start.46
  1041.1 1.4 copy-start.12
  1132.3 113.8 %reduce-scatter.22.cloned.1.call-start = ((), (), s32[]{:S(2)}) async-start(), calls=%async_computation.20 | async-start | bytes 442368
  1133.3 4.6 copy-start.48
  1133.3 4.7 copy-start.47
  1139.0 149.7 %all-gather.17.cloned.1.call-start = ((), (), s32[]{:S(2)}) async-start(), calls=%async_computation.15 | async-start | bytes 1327104 | tf_op jit(solution)/shard_map/all_gather | solution.py:220
  1180.5 150.3 %all-gather.13.cloned.1.call-start = ((), (), s32[]{:S(2)}) async-start(), calls=%async_computation.11 | async-start | bytes 1327104 | tf_op jit(solution)/shard_map/all_gather | solution.py:214
  1181.1 203.0 %all-gather.15.cloned.1.call-start = ((), (), s32[]{:S(2)}) async-start(), calls=%async_computation.13 | async-start | bytes 2654208 | tf_op jit(solution)/shard_map/all_gather | solution.py:217
  1181.8 283.0 %all-gather.21.cloned.1.call-start = ((), (), s32[]{:S(2)}) async-start(), calls=%async_computation.19 | async-start | bytes 5308416 | tf_op jit(solution)/shard_map/all_gather | solution.py:226
  1182.4 362.7 %all-gather.19.cloned.1.call-start = ((), (), s32[]{:S(2)}) async-start(), calls=%async_computation.17 | async-start | bytes 5308416 | tf_op jit(solution)/shard_map/all_gather | solution.py:223
  1193.4 2.5 copy-start.14
  1545.1 7.5 copy-start.1
  (18 other events, 18.4 us)
Sparse Core Ops, SparseCore 0:
  19.0 40.1 all-gather.10
  61.3 37.4 all-gather.8
  290.7 264.7 reduce-scatter.9
  558.8 69.1 reduce-scatter.15
  631.3 68.2 reduce-scatter.11
  703.1 162.4 reduce-scatter.19
  869.2 162.5 reduce-scatter.17
  1036.0 94.4 reduce-scatter.13
  1133.8 46.5 all-reduce.2
  1184.5 61.5 reduce-scatter.21
  1248.5 40.0 all-gather.16
  1290.9 39.8 all-gather.12
  1333.2 50.8 all-gather.14
  1386.4 78.4 all-gather.20
  1467.1 78.0 all-gather.18
where the time goes:
time: 1570 us; the launch traced here: 1560 us
  waiting for transfers between devices  1190 us (76%)
  local copies, waits for them, and re-layouts  128 us (8%)
  matrix products  123 us (8%)
  other arithmetic  55.5 us (4%)
  blocking collectives  31.8 us (2%)
    reduce_scatter x1, waiting for transfers between devices, attention_backward(): lax.psum_scatter(kv_terms.astype(jnp.bfloat16), 'pass', scatter_dimension...  231 us
    reduce_scatter x1, waiting for transfers between devices, on_device(): lax.psum_scatter(grad_w_down, 'dp', scatter_dimension=0, tiled=True)  164 us
    reduce_scatter x1, waiting for transfers between devices, on_device(): lax.psum_scatter(grad_w_up, 'dp', scatter_dimension=0, tiled=True)  164 us
    reduce_scatter x1, waiting for transfers between devices, on_device(): lax.psum_scatter(grad_w_keyval, 'dp', scatter_dimension=0, tiled=True)  86.7 us
    all_gather x1, waiting for transfers between devices, on_device(): lax.all_gather(share_down.astype(jnp.bfloat16), 'dp', axis=0, tiled=True)  75.3 us
    all_gather x1, waiting for transfers between devices, on_device(): lax.all_gather(share_up.astype(jnp.bfloat16), 'dp', axis=0, tiled=True)  73.5 us
    reduce_scatter x1, waiting for transfers between devices, on_device(): lax.psum_scatter(grad_w_query, 'dp', scatter_dimension=0, tiled=True)  70 us
    reduce_scatter x1, waiting for transfers between devices, on_device(): lax.psum_scatter(grad_w_out, 'dp', scatter_dimension=0, tiled=True)  64.6 us
  transfers between devices with their start and end apart: 15, of which 15 were waited for; matrix products, arithmetic and copies ran while one was open for 6% of the time, Pallas kernels for 0%

commit v1 on v0

v1 whole, which is shorter than its diff:
```python
import functools
import math

import jax
import jax.numpy as jnp
from jax import lax
from jax.experimental import pallas as pl
from jax.experimental.pallas import tpu as pltpu
from jax.sharding import PartitionSpec as P

D = 768
HEADS = 12
HEAD_DIM = 64
SHORT = 256
GROUP = D // 2
HALF = GROUP // 2
EPS = 1e-05
SCALE = HEAD_DIM**-0.5
SCALE2 = SCALE * math.log2(math.e)
BF = jnp.bfloat16
F32 = jnp.float32


def dot(a, b, ca, cb):
    return lax.dot_general(a, b, (((ca,), (cb,)), ((), ())), preferred_element_type=F32)


def mask_tail(scores):
    n = scores.shape[0]
    key = lax.broadcasted_iota(jnp.int32, (SHORT, SHORT), 0)
    query = lax.broadcasted_iota(jnp.int32, (SHORT, SHORT), 1)
    diag = jnp.where(key <= query, scores[n - SHORT :], -1e30)
    return diag if n == SHORT else jnp.concatenate([scores[: n - SHORT], diag], 0)


def over_tiles(flag_ref, tiles, cross, tile):
    one_sequence = flag_ref[0] == 1
    even = 0 if cross else flag_ref[1]
    odd = 1 - even

    def run(whole):
        for at in range(tiles):
            first = 0 if whole else at
            tile(even, at, [even, odd] if cross else [even], first)
            tile(odd, at, [even, odd], first)

    pl.when(one_sequence)(lambda: run(True))
    pl.when(jnp.logical_not(one_sequence))(lambda: run(False))


def forward_kernel(flag_ref, q_ref, k_ref, v_ref, o_ref, lse_ref, *, cross):
    def tile(qp, at, keys, first):
        qs, ks = slice(at * SHORT, (at + 1) * SHORT), slice(first * SHORT, (at + 1) * SHORT)
        q = q_ref[qp, :, qs]
        scores = [mask_tail(dot(k_ref[kp, :, ks], q, 0, 0) * SCALE2) for kp in keys]
        top = functools.reduce(
            jnp.maximum, [jnp.max(s, axis=0, keepdims=True) for s in scores]
        )
        raw = [jnp.exp2(s - top) for s in scores]
        total = functools.reduce(jnp.add, [jnp.sum(p, axis=0, keepdims=True) for p in raw])
        out = functools.reduce(
            jnp.add, [dot(v_ref[kp, :, ks], p.astype(BF), 1, 0) for kp, p in zip(keys, raw)]
        )
        o_ref[qp, :, qs] = out * (1.0 / total)
        lse_ref[0, pl.ds(qp, 1), qs] = top + jnp.log2(total)

    over_tiles(flag_ref, q_ref.shape[2] // SHORT, cross, tile)


def backward_kernel(
    flag_ref, q_ref, k_ref, v_ref, g_ref, lse_ref, delta_ref, dq_ref, dk_ref, dv_ref, dk_acc, dv_acc, *, cross
):
    dk_acc[...] = jnp.zeros_like(dk_acc)
    dv_acc[...] = jnp.zeros_like(dv_acc)

    def tile(qp, at, keys, first):
        qs, ks = slice(at * SHORT, (at + 1) * SHORT), slice(first * SHORT, (at + 1) * SHORT)
        q, g = q_ref[qp, :, qs], g_ref[qp, :, qs]
        lse, delta = lse_ref[0, pl.ds(qp, 1), qs], delta_ref[0, pl.ds(qp, 1), qs]
        dq = None
        for kp in keys:
            k, v = k_ref[kp, :, ks], v_ref[kp, :, ks]
            weights = jnp.exp2(mask_tail(dot(k, q, 0, 0) * SCALE2) - lse)
            ds = (weights * (dot(v, g, 0, 0) - delta)).astype(BF)
            term = dot(k, ds, 1, 0)
            dq = term if dq is None else dq + term
            dk_acc[kp, :, ks] += dot(q, ds, 1, 1)
            dv_acc[kp, :, ks] += dot(g, weights.astype(BF), 1, 1)
        dq_ref[qp, :, qs] = (dq * SCALE).astype(dq_ref.dtype)

    over_tiles(flag_ref, q_ref.shape[2] // SHORT, cross, tile)
    dk_ref[...] = (dk_acc[...] * SCALE).astype(dk_ref.dtype)
    dv_ref[...] = dv_acc[...].astype(dv_ref.dtype)


def head_spec(length, part, heads):
    return pl.BlockSpec((2, HEAD_DIM, length), lambda h, flags: (0, part * heads + h, 0))


def row_spec(length):
    return pl.BlockSpec((1, 2, length), lambda h, flags: (h, 0, 0))


def attend(flags, queries, keys, values, cross):
    length, heads = queries[0].shape[2], HEADS // 4 if cross else HEADS // 2
    rows = heads * HEAD_DIM
    units = 4 if cross else 3
    flops = 4 * units * heads * length * length * HEAD_DIM
    return pl.pallas_call(
        functools.partial(forward_kernel, cross=cross),
        grid_spec=pltpu.PrefetchScalarGridSpec(
            num_scalar_prefetch=1,
            grid=(heads,),
            in_specs=[head_spec(length, part, heads) for _, part in (queries, keys, values)],
            out_specs=[head_spec(length, 0, heads), row_spec(length)],
        ),
        out_shape=[
            jax.ShapeDtypeStruct((2, rows, length), F32),
            jax.ShapeDtypeStruct((heads, 2, length), F32),
        ],
        cost_estimate=pl.CostEstimate(
            flops=4 * flops, bytes_accessed=2 * rows * length * 10, transcendentals=0
        ),
        compiler_params=pltpu.CompilerParams(vmem_limit_bytes=40 << 20),
        name="attend_cross" if cross else "attend_local",
    )(flags, queries[0], keys[0], values[0])


def attend_back(flags, queries, keys, values, grads, lse, delta, cross, out_type):
    length, heads = queries[0].shape[2], HEADS // 4 if cross else HEADS // 2
    rows = heads * HEAD_DIM
    units = 4 if cross else 3
    flops = 10 * units * heads * length * length * HEAD_DIM
    return pl.pallas_call(
        functools.partial(backward_kernel, cross=cross),
        grid_spec=pltpu.PrefetchScalarGridSpec(
            num_scalar_prefetch=1,
            grid=(heads,),
            in_specs=[
                head_spec(length, part, heads) for _, part in (queries, keys, values, grads)
            ]
            + [row_spec(length)] * 2,
            out_specs=[head_spec(length, 0, heads)] * 3,
            scratch_shapes=[pltpu.VMEM((2, HEAD_DIM, length), F32)] * 2,
        ),
        out_shape=[jax.ShapeDtypeStruct((2, rows, length), out_type)] * 3,
        cost_estimate=pl.CostEstimate(
            flops=3 * flops, bytes_accessed=2 * rows * length * 20, transcendentals=0
        ),
        compiler_params=pltpu.CompilerParams(vmem_limit_bytes=40 << 20),
        name="attend_back_cross" if cross else "attend_back_local",
    )(flags, queries[0], keys[0], values[0], grads[0], lse, delta)


def swap(array, step):
    axis, mask, size = step
    return lax.ppermute(array, axis, [(i, i ^ mask) for i in range(size)])


def side(step):
    axis, mask, _ = step
    return (lax.axis_index(axis) // mask) % 2


def halve(total, step):
    here, half = side(step), total.shape[0] // 2
    sent = lax.dynamic_slice_in_dim(total, (1 - here) * half, half, 0).astype(BF)
    kept = lax.dynamic_slice_in_dim(total, here * half, half, 0)
    return kept + swap(sent, step).astype(F32)


def join(own, other, step, axis=0):
    return jnp.where(
        side(step) == 0,
        jnp.concatenate([own, other], axis),
        jnp.concatenate([other, own], axis),
    )


def sum_over(total, steps):
    for step in steps:
        total = halve(total, step)
    total = total.astype(BF)
    for step in reversed(steps):
        total = join(total, swap(total, step), step)
    return total


def on_device(
    sizes, block_input, segments, pass_emb, gain_attn, w_qkv, w_out, gain_mlp, w_up, w_down, cotangent
):
    passes, n_dp = sizes
    core = ("pass", 1, passes)
    cross = ("pass", 2, passes)
    lanes = [("dp", 1 << i, n_dp) for i in range(n_dp.bit_length() - 1)]
    order_a = [cross] + lanes
    order_b = lanes[:1] + [cross] + lanes[1:]
    order_c = lanes[1:] + [cross] + lanes[:1]

    pass_here = lax.axis_index("pass")
    core_here = pass_here % 2
    early = pass_here < 2
    to_late = [(0, 2), (1, 3)]
    to_early = [(2, 0), (3, 1)]
    length = segments.shape[0]
    one_sequence = (segments[0] == segments[length - 1]).astype(jnp.int32)
    flags = jnp.stack([one_sequence, core_here.astype(jnp.int32)])

    emb_row = lax.dynamic_index_in_dim(pass_emb, pass_here, 0, keepdims=False)
    hidden = block_input[0].astype(F32) + emb_row
    center = hidden - jnp.mean(hidden, axis=-1, keepdims=True)
    inv_attn = lax.rsqrt(jnp.mean(center * center, axis=-1, keepdims=True) + EPS)
    normed = (center * inv_attn * gain_attn).astype(BF)
    projected = dot(w_qkv, normed, 0, 1).astype(BF).reshape(3, 2, GROUP, length)

    own = lax.dynamic_index_in_dim(projected, core_here, 1, keepdims=False)
    theirs = lax.dynamic_index_in_dim(projected, 1 - core_here, 1, keepdims=False)
    pair = jnp.stack([own, swap(theirs, core)])
    normed_partner = swap(normed, core)
    kv_late = lax.ppermute(pair[:, 1:, :HALF], "pass", to_late)
    q_early = lax.ppermute(pair[:, 0, HALF:], "pass", to_early)
    flat = pair.reshape(2, 3 * GROUP, length)
    out_local, lse_local = attend(flags, (flat, 0), (flat, 1), (flat, 2), False)
    q_cross = jnp.where(early, q_early, pair[:, 0, :HALF])
    kv_cross = jnp.where(early, pair[:, 1:, HALF:], kv_late).reshape(2, 2 * HALF, length)
    out_cross, lse_cross = attend(flags, (q_cross, 0), (kv_cross, 0), (kv_cross, 1), True)
    out_back = lax.ppermute(out_cross.astype(BF), "pass", to_late)
    lse_back = lax.ppermute(lse_cross, "pass", to_late)

    lse_other = jnp.concatenate([lse_cross, lse_back], 0)
    out_other = jnp.concatenate([out_cross, out_back.astype(F32)], 1)
    top = jnp.maximum(lse_local, lse_other)
    lse_both = top + jnp.log2(jnp.exp2(lse_local - top) + jnp.exp2(lse_other - top))
    lse = jnp.where(early, lse_local, lse_both)
    share_local = jnp.where(early, 1.0, jnp.exp2(lse_local - lse)).transpose(1, 0, 2)[:, :, None]
    share_other = jnp.where(early, 0.0, jnp.exp2(lse_other - lse_both)).transpose(1, 0, 2)[:, :, None]
    by_head = (2, HEADS // 2, HEAD_DIM, length)
    attended_f32 = (
        out_local.reshape(by_head) * share_local + out_other.reshape(by_head) * share_other
    )
    attended_pair = attended_f32.reshape(2, GROUP, length).astype(BF)
    attended = join(attended_pair[0], swap(attended_pair[1], core), core)

    residual = hidden + dot(attended, w_out, 0, 0)
    center2 = residual - jnp.mean(residual, axis=-1, keepdims=True)
    inv_mlp = lax.rsqrt(jnp.mean(center2 * center2, axis=-1, keepdims=True) + EPS)
    n2 = center2 * inv_mlp
    normed2 = (n2 * gain_mlp).astype(BF)
    up_proj = dot(normed2, w_up, 1, 0)
    activated_val, gelu_pull = jax.vjp(lambda u: jax.nn.gelu(u, approximate=True), up_proj)
    activated = activated_val.astype(BF)
    output = (residual + dot(activated, w_down, 1, 0)).astype(BF)

    grad_out = cotangent[0]
    ff_half = activated.shape[1] // 2

    def columns(array, which, width):
        return lax.dynamic_slice_in_dim(array, which * width, width, 1)

    down_sent = dot(columns(activated, 1 - core_here, ff_half), grad_out, 0, 0).astype(BF)
    down_recv = swap(down_sent, core)
    grad_up = gelu_pull(dot(grad_out, w_down, 1, 1))[0].astype(BF)
    down_half = dot(columns(activated, core_here, ff_half), grad_out, 0, 0) + down_recv.astype(F32)
    up_sent = dot(columns(normed2, 1 - core_here, GROUP), grad_up, 0, 0).astype(BF)
    up_recv = swap(up_sent, core)
    grad_normed2 = dot(grad_up, w_up, 1, 1)
    up_half = dot(columns(normed2, core_here, GROUP), grad_up, 0, 0) + up_recv.astype(F32)
    grad_gain_mlp = jnp.sum(grad_normed2 * n2, axis=0)
    scaled = grad_normed2 * gain_mlp
    grad_residual = grad_out.astype(F32) + inv_mlp * (
        scaled
        - jnp.mean(scaled, axis=-1, keepdims=True)
        - n2 * jnp.mean(scaled * n2, axis=-1, keepdims=True)
    )
    grad_attn = grad_residual.astype(BF)

    grad_attn_pair = jnp.stack([grad_attn, swap(grad_attn, core)])
    w_out_half = lax.dynamic_slice_in_dim(w_out, core_here * GROUP, GROUP, 0)
    grad_attended = jnp.stack(
        [dot(w_out_half, grad_attn_pair[i], 1, 1) for i in range(2)]
    ).astype(BF)
    delta = jnp.sum(grad_attended.astype(F32).reshape(by_head) * attended_f32, axis=2).transpose(
        1, 0, 2
    )
    half_heads = HEADS // 4
    grad_early = lax.ppermute(grad_attended[:, HALF:], "pass", to_early)
    rows_early = lax.ppermute(
        jnp.stack([lse[half_heads:], delta[half_heads:]]), "pass", to_early
    )
    out_half = dot(attended_pair[0], grad_attn_pair[0], 1, 0) + dot(
        attended_pair[1], grad_attn_pair[1], 1, 0
    )
    dq_local, dk_local, dv_local = attend_back(
        flags, (flat, 0), (flat, 1), (flat, 2), (grad_attended, 0), lse, delta, False, F32
    )
    grad_cross = jnp.where(early, grad_early, grad_attended[:, :HALF])
    lse_x = jnp.where(early, rows_early[0], lse[:half_heads])
    delta_x = jnp.where(early, rows_early[1], delta[:half_heads])
    dq_cross, dk_cross, dv_cross = attend_back(
        flags, (q_cross, 0), (kv_cross, 0), (kv_cross, 1), (grad_cross, 0), lse_x, delta_x, True, BF
    )
    dq_back = lax.ppermute(dq_cross, "pass", to_late)
    dkv_back = lax.ppermute(jnp.stack([dk_cross, dv_cross]), "pass", to_early)
    dq = dq_local + jnp.where(
        early, 0.0, jnp.concatenate([dq_cross, dq_back], 1).astype(F32)
    )
    dk = dk_local + jnp.where(
        early, jnp.concatenate([dkv_back[0], dk_cross], 1).astype(F32), 0.0
    )
    dv = dv_local + jnp.where(
        early, jnp.concatenate([dkv_back[1], dv_cross], 1).astype(F32), 0.0
    )
    grad_pair = jnp.stack([dq, dk, dv], 1).astype(BF)
    grad_other = swap(grad_pair[1], core)
    parts = [
        dot(normed, grad_pair[0, i], 0, 1) + dot(normed_partner, grad_pair[1, i], 0, 1)
        for i in range(3)
    ]

    grad_normed = jnp.zeros((length, D), F32)
    w_by_core = w_qkv.reshape(D, 3, 2, GROUP)
    w_own = lax.dynamic_index_in_dim(w_by_core, core_here, 2, keepdims=False).reshape(D, 3 * GROUP)
    w_other = lax.dynamic_index_in_dim(w_by_core, 1 - core_here, 2, keepdims=False).reshape(
        D, 3 * GROUP
    )
    grad_normed = dot(grad_pair[0].reshape(3 * GROUP, length), w_own, 0, 1) + dot(
        grad_other.reshape(3 * GROUP, length), w_other, 0, 1
    )
    n1 = center * inv_attn
    grad_gain_attn = jnp.sum(grad_normed * n1, axis=0)
    scaled1 = grad_normed * gain_attn
    grad_hidden = grad_residual + inv_attn * (
        scaled1
        - jnp.mean(scaled1, axis=-1, keepdims=True)
        - n1 * jnp.mean(scaled1 * n1, axis=-1, keepdims=True)
    )
    selector = (jnp.arange(passes) == pass_here).astype(F32)
    small = jnp.concatenate(
        [
            selector[:, None] * jnp.sum(grad_hidden, axis=0)[None],
            grad_gain_attn[None],
            grad_gain_mlp[None],
        ]
    )
    for step in [core, cross] + lanes:
        small = small + swap(small, step)

    def whole(half, steps, axis=0):
        half = sum_over(half, steps)
        return join(half, swap(half, core), core, axis).astype(F32)

    down_total = whole(down_half, order_a)
    up_total = whole(up_half, order_b)
    out_total = whole(out_half, order_c)
    qkv_total = jnp.concatenate(
        [
            whole(part, order, 1)
            for part, order in zip(parts, (order_a, order_b, order_c), strict=True)
        ],
        axis=1,
    )
    return (
        output[None],
        grad_hidden.astype(BF)[None],
        small[:passes],
        small[passes],
        qkv_total,
        out_total,
        small[passes + 1],
        up_total,
        down_total,
    )


def solution(mesh):
    sizes = (mesh.shape["pass"], mesh.shape["dp"])
    tokens = P("pass", "dp", None)
    in_specs = (tokens, P("dp")) + (P(),) * 7 + (tokens,)
    out_specs = (tokens, tokens) + (P(),) * 7
    return jax.shard_map(
        functools.partial(on_device, sizes),
        mesh=mesh,
        in_specs=in_specs,
        out_specs=out_specs,
        check_vma=False,
    )
```

time: 1570 us -> 567 us (0.36)
  waiting for transfers between devices: 1190 us -> 220 us
  starting transfers between devices: 1.36 us -> 95.1 us
  local copies, waits for them, and re-layouts: 128 us -> 70.6 us
  matrix products: 123 us -> 72.9 us
  Pallas kernels: 0 us -> 45.7 us
  blocking collectives: 31.8 us -> 0 us
    reduce_scatter x6 -> x0, waiting for transfers between devices: 781 us -> none  [the longest x1 231 us: attention_backward(): lax.psum_scatter(kv_terms.astype(jnp.bfloat16), 'pass', scatter_dimension...]
    all_gather x7 -> x0, waiting for transfers between devices: 319 us -> none  [the longest x1 75.3 us: on_device(): lax.all_gather(share_down.astype(jnp.bfloat16), 'dp', axis=0, tiled=True)]
    ppermute x0 -> x74, waiting for transfers between devices: none -> 220 us  [the longest x66 192 us: swap(): return lax.ppermute(array, axis, [(i, i ^ mask) for i in range(size)])]
    ppermute x0 -> x74, starting transfers between devices: none -> 95.1 us  [the longest x66 76.9 us: swap(): return lax.ppermute(array, axis, [(i, i ^ mask) for i in range(size)])]
    dynamic_update_slice x24 -> x0, local copies, waits for them, and re-layouts: 52.2 us -> none  [attention_backward(): grad_queries, pieces = lax.scan(sweep_step, start, jnp.arange(total_blocks))]
    unnamed x16 -> x0, waiting for transfers between devices: 51.9 us -> none
    dot_general x35 -> x22, matrix products: 123 us -> 72.9 us  [dot(): lax.dot_general(a, b, (((ca,), (cb,)), ((), ())), preferred_element_type=...]
    pallas_call x0 -> x4, Pallas kernels: none -> 45.7 us  [the longest x2 28.9 us: attend_back(): pl.pallas_call(functools.partial(backward_kernel, cross=cross), grid_spec...]
  transfers between devices with their start and end apart: 15 -> 74, of which waited for: 15 -> 38; matrix products, arithmetic and copies ran while one was open for 6% -> 25% of each run, Pallas kernels for 0% -> 8%
where the time goes in v1:
time: 567 us; the launch traced here: 558 us
  waiting for transfers between devices  220 us (39%)
  starting transfers between devices  95.1 us (17%)
  matrix products  72.9 us (13%)
  local copies, waits for them, and re-layouts  70.6 us (12%)
  other arithmetic  50 us (9%)
  Pallas kernels  45.7 us (8%)
    ppermute x66, waiting for transfers between devices, swap(): return lax.ppermute(array, axis, [(i, i ^ mask) for i in range(size)])  192 us
    ppermute x66, starting transfers between devices, swap(): return lax.ppermute(array, axis, [(i, i ^ mask) for i in range(size)])  76.9 us
    dot_general x22, matrix products, dot(): lax.dot_general(a, b, (((ca,), (cb,)), ((), ())), preferred_element_type=...  72.9 us
    unnamed x126, local copies, waits for them, and re-layouts  39.4 us
    pallas_call x2, Pallas kernels, attend_back(): pl.pallas_call(functools.partial(backward_kernel, cross=cross), grid_spec...  28.9 us
    pallas_call x2, Pallas kernels, attend(): pl.pallas_call(functools.partial(forward_kernel, cross=cross), grid_spec=...  16.8 us
    convert_element_type x3, other arithmetic, whole(): return join(half, swap(half, core), core, axis).astype(F32)  16.5 us
    dynamic_slice x1, local copies, waits for them, and re-layouts, on_device(): own = lax.dynamic_index_in_dim(projected, core_here, 1, keepdims=False)  13.3 us
  transfers between devices with their start and end apart: 74, of which 38 were waited for; matrix products, arithmetic and copies ran while one was open for 25% of the time, Pallas kernels for 8%

profile of v1, /device:TPU:0, one launch (start us, length us, event | category | flops | bytes accessed | tf_op | source)
XLA Modules:
  0.0 557.8 jit_solution(1724291233525137595)
XLA Ops:
  5.5 6.0 %fusion.9 = bf16[2304,768]{0,1:T(8,128)(2,1)} fusion(bf16[768,768]{0,1:T(8,128)(2,1)} %fusion.20, bf16[768,2304]{1,0:T(8,128)(2,1)S(1)} %copy-done.26), kind=kOutput, calls=%fused_computation.17 | convolution fusion | flops 2719678464 | bytes 8257536 | tf_op jit(solution)/shard_map/dot_general | solution.py:25
  11.4 7.7 %reshape.205 = bf16[3,2,384,768]{2,1,0,3:T(2,128)(2,1)} reshape(bf16[2304,768]{0,1:T(8,128)(2,1)} %fusion.9) | data formatting | bytes 7077888 | tf_op jit(solution)/shard_map/reshape | solution.py:214
  19.2 13.3 %constant_dynamic-slice_fusion.3 = (bf16[3,1,384,768]{2,1,0,3:T(2,128)(2,1)}, bf16[3,1,384,768]{2,1,0,3:T(2,128)(2,1)}) fusion(bf16[3,2,384,768]{2,1,0,3:T(2,128)(2,1)} %reshape.205, s32[]{:T(128)S(6)} %select_n.603, s32[]{:T(128)S(6)} %select_n.604), kind=kLoop, calls=%fused_computation.223 | loop fusion | bytes 7077896 | tf_op jit(solution)/shard_map/jit(dynamic_index_in_dim)/dynamic_slice | solution.py:216
  32.5 11.8 %copy.82 = bf16[3,1,384,768]{3,2,0,1:T(8,128)(2,1)} copy(bf16[3,1,384,768]{2,1,0,3:T(2,128)(2,1)} %get-tuple-element.82) | data formatting | bytes 3538944
  44.9 5.7 %copy.71 = bf16[768,2304]{0,1:T(8,128)(2,1)} copy(bf16[768,2304]{1,0:T(8,128)(2,1)} %param.14) | data formatting | bytes 7077888 | tf_op args[4]
  53.3 9.9 %copy.81 = bf16[3,1,384,768]{3,2,0,1:T(8,128)(2,1)S(1)} copy(bf16[3,1,384,768]{2,1,0,3:T(2,128)(2,1)} %get-tuple-element.81) | data formatting | bytes 3538944
  63.2 2.9 copy.68
  66.2 4.0 constant_dynamic-slice_fusion
  73.7 4.9 collective-permute-start.2
  80.5 9.8 %attend_local.1 = (f32[2,384,768]{2,1,0:T(8,128)S(1)}, f32[6,2,768]{2,1,0:T(2,128)S(1)}) custom-call(s32[2]{0:T(128)S(1)} %pad_add_fusion.flag_ref, bf16[2,1152,768]{2,1,0:T(8,128)(2,1)S(1)} %pad_maximum_fusion.q_ref.k_ref.v_ref, bf16[2,1152,768]{2,1,0:T(8,128)(2,1)S(1)} %pad_maximum_fusion.q_ref.k_ref.v_ref, ...), custom_call_target="tpu_custom_call" | custom-call | flops 10871635968 | bytes 5898240 | tf_op jit(solution)/shard_map/attend_local/pallas_call | solution.py:109
  91.4 12.6 %collective-permute-done.2 = bf16[2,2,192,768]{3,2,0,1:T(8,128)(2,1)S(1)} collective-permute-done((bf16[2,2,192,768]{3,2,0,1:T(8,128)(2,1)S(1)}, bf16[2,2,192,768]{3,2,0,1:T(8,128)(2,1)S(1)}, u32[]{:S(2)}, u32[]{:S(2)}) %collective-permute-start.2) | collective-permute-done | bytes 1179680 | tf_op jit(solution)/shard_map/ppermute | solution.py:220
  105.5 7.0 %attend_cross.1 = (f32[2,192,768]{2,1,0:T(8,128)S(1)}, f32[3,2,768]{2,1,0:T(2,128)S(1)}) custom-call(s32[2]{0:T(128)S(1)} %pad_add_fusion.flag_ref, bf16[2,192,768]{2,1,0:T(8,128)(2,1)S(1)} %fusion.59.q_ref, bf16[2,384,768]{2,1,0:T(8,128)(2,1)S(1)} %bitcast.183, bf16[2,384,768]{2,1,0:T(8,128)(2,1)S(1)} %bitcast.184), custom_call_target="tpu_custom_call" | custom-call | flops 7247757312 | bytes 2949120 | tf_op jit(solution)/shard_map/attend_cross/pallas_call | solution.py:109
  112.6 4.4 collective-permute-start.4
  118.5 10.8 %collective-permute-done.3 = f32[3,2,768]{2,1,0:T(2,128)S(1)} collective-permute-done((f32[3,2,768]{2,1,0:T(2,128)S(1)}, f32[3,2,768]{2,1,0:T(2,128)S(1)}, u32[]{:S(2)}, u32[]{:S(2)}) %collective-permute-start.3) | collective-permute-done | bytes 18464 | tf_op jit(solution)/shard_map/ppermute | solution.py:228
  137.8 8.4 %multiply_convert_fusion = (bf16[768,3072]{1,0:T(8,128)(2,1)S(1)}, f32[768,3072]{1,0:T(8,128)}) fusion(bf16[768,768]{0,1:T(8,128)(2,1)S(1)} %multiply_convert_fusion.1, bf16[768,3072]{1,0:T(8,128)(2,1)S(1)} %bitcast.217), kind=kOutput, calls=%fused_computation.9 | convolution fusion | flops 3645112320 | bytes 20054016 | tf_op jit(solution)/shard_map/dot_general | solution.py:25
  146.2 5.3 fusion.38
  151.5 11.3 %fusion.6 = bf16[768,3072]{1,0:T(8,128)(2,1)S(1)} fusion(f32[768,3072]{1,0:T(8,128)} %get-tuple-element.98, bf16[3072,768]{1,0:T(8,128)(2,1)S(1)} %bitcast.215, bf16[1,768,768]{2,1,0:T(8,128)(2,1)S(1)} %copy-done.31), kind=kOutput, calls=%fused_computation.8 | convolution fusion | flops 3671064576 | bytes 20054016 | tf_op jit(solution)/shard_map/dot_general | solution.py:25
  162.8 4.9 multiply_reduce_fusion
  169.7 3.5 convolution_convert_fusion.1
  176.7 5.4 convolution_convert_fusion.2
  188.2 5.8 %collective-permute-start.45 = (bf16[192,768]{1,0:T(8,128)(2,1)S(1)}, bf16[192,768]{1,0:T(8,128)(2,1)S(1)}, u32[]{:S(2)}, u32[]{:S(2)}) collective-permute-start(bf16[192,768]{1,0:T(8,128)(2,1)S(1)} %dynamic-slice_convert_fusion.6), channel_id=1, source_target_pairs={{0,2},{1,3},{2,0},{3,1},{4,6},{5,7},{6,4},{7,5},{8,10},{9,11},{10,... | collective-permute-start | bytes 884744 | tf_op jit(solution)/shard_map/ppermute | solution.py:157
  198.0 3.5 collective-permute-done.45
  204.3 7.0 %collective-permute-done.46 = bf16[96,768]{1,0:T(8,128)(2,1)S(1)} collective-permute-done((bf16[96,768]{1,0:T(8,128)(2,1)S(1)}, bf16[96,768]{1,0:T(8,128)(2,1)S(1)}, u32[]{:S(2)}, u32[]{:S(2)}) %collective-permute-start.46) | collective-permute-done | bytes 147488 | tf_op jit(solution)/shard_map/ppermute | solution.py:157
  221.6 4.5 collective-permute-done.8
  230.3 4.2 collective-permute-done.50
  236.6 11.2 %attend_back_cross.1 = (bf16[2,192,768]{2,1,0:T(8,128)(2,1)S(1)}, bf16[2,192,768]{2,1,0:T(8,128)(2,1)S(1)}, bf16[2,192,768]{2,1,0:T(8,128)(2,1)S(1)}) custom-call(s32[2]{0:T(128)S(1)} %pad_add_fusion.flag_ref, bf16[2,192,768]{2,1,0:T(8,128)(2,1)S(1)} %copy-done.7, bf16[2,384,768]{2,1,0:T(8,128)(2,1)S(1)} %bitcast.185, bf16[2,384,768]{2,1,0:T(8,128)(2,1)S(1)} %bitcast.186, ...), custom_call_target="tpu_custom_call" | custom-call | flops 13589544960 | bytes 5898240 | tf_op jit(solution)/shard_map/attend_back_cross/pallas_call | solution.py:134
  249.8 7.7 %collective-permute-start.52 = (bf16[192,768]{1,0:T(8,128)(2,1)S(1)}, bf16[192,768]{1,0:T(8,128)(2,1)S(1)}, u32[]{:S(2)}, u32[]{:S(2)}) collective-permute-start(bf16[192,768]{1,0:T(8,128)(2,1)S(1)} %maximum_select_fusion.22), channel_id=1, source_target_pairs={{0,2},{1,3},{2,0},{3,1},{4,6},{5,7},{6,4},{7,5},{8,10},{9,11},{10,... | collective-permute-start | bytes 884744 | tf_op jit(solution)/shard_map/ppermute | solution.py:157
  257.5 17.7 %attend_back_local.1 = (f32[2,384,768]{2,1,0:T(8,128)S(1)}, f32[2,384,768]{2,1,0:T(8,128)S(1)}, f32[2,384,768]{2,1,0:T(8,128)S(1)}) custom-call(s32[2]{0:T(128)S(1)} %pad_add_fusion.flag_ref, bf16[2,1152,768]{2,1,0:T(8,128)(2,1)S(1)} %copy-done.3, bf16[2,1152,768]{2,1,0:T(8,128)(2,1)S(1)} %copy-done.3, bf16[2,1152,768]{2,1,0:T(8,128)(2,1)S(1)} %copy-done.3, ...), custom_call_target="tpu_custom_call" | custom-call | flops 20384317440 | bytes 11796480 | tf_op jit(solution)/shard_map/attend_back_local/pallas_call | solution.py:134
  281.4 2.8 collective-permute-start.18
  286.2 19.8 %collective-permute-done.18 = bf16[384,384]{1,0:T(8,128)(2,1)S(1)} collective-permute-done((bf16[384,384]{1,0:T(8,128)(2,1)S(1)}, bf16[384,384]{1,0:T(8,128)(2,1)S(1)}, u32[]{:S(2)}, u32[]{:S(2)}) %collective-permute-start.18) | collective-permute-done | bytes 294944 | tf_op jit(solution)/shard_map/ppermute | solution.py:157
  306.1 6.3 %collective-permute-start.19 = (bf16[192,384]{1,0:T(8,128)(2,1)S(1)}, bf16[192,384]{1,0:T(8,128)(2,1)S(1)}, u32[]{:S(2)}, u32[]{:S(2)}) collective-permute-start(bf16[192,384]{1,0:T(8,128)(2,1)S(1)} %dynamic-slice_convert_fusion.15), channel_id=1, source_target_pairs={{0,1},{1,0},{2,3},{3,2},{4,5},{5,4},{6,7},{7,6},{8,9},{9,8},{10,11... | collective-permute-start | bytes 442376 | tf_op jit(solution)/shard_map/ppermute | solution.py:157
  312.6 4.5 collective-permute-done.19
  317.2 4.0 collective-permute-start.20
  321.2 3.8 convert_add_fusion
  325.6 4.7 collective-permute-done.21
  343.7 3.0 collective-permute-done.24
  347.7 5.8 %collective-permute-done.27 = bf16[384,384]{1,0:T(8,128)(2,1)S(1)} collective-permute-done((bf16[384,384]{1,0:T(8,128)(2,1)S(1)}, bf16[384,384]{1,0:T(8,128)(2,1)S(1)}, u32[]{:S(2)}, u32[]{:S(2)}) %collective-permute-start.27) | collective-permute-done | bytes 294944 | tf_op jit(solution)/shard_map/ppermute | solution.py:157
  353.4 3.2 collective-permute-start.37
  356.8 4.6 collective-permute-done.37
  361.4 5.5 collective-permute-done.28
  367.3 4.0 collective-permute-done.38
  371.3 4.3 collective-permute-done.29
  376.8 2.8 collective-permute-done.39
  387.0 8.2 %collective-permute-done.56 = bf16[96,3072]{1,0:T(8,128)(2,1)S(1)} collective-permute-done((bf16[96,3072]{1,0:T(8,128)(2,1)S(1)}, bf16[96,3072]{1,0:T(8,128)(2,1)S(1)}, u32[]{:S(2)}, u32[]{:S(2)}) %collective-permute-start.56) | collective-permute-done | bytes 589856 | tf_op jit(solution)/shard_map/ppermute | solution.py:157
  395.7 4.0 collective-permute-done.41
  400.4 5.8 %collective-permute-done.32 = bf16[96,384]{1,0:T(8,128)(2,1)S(1)} collective-permute-done((bf16[96,384]{1,0:T(8,128)(2,1)S(1)}, bf16[96,384]{1,0:T(8,128)(2,1)S(1)}, u32[]{:S(2)}, u32[]{:S(2)}) %collective-permute-start.32) | collective-permute-done | bytes 73760 | tf_op jit(solution)/shard_map/ppermute | solution.py:157
  408.6 3.0 collective-permute-start.58
  411.7 7.5 %collective-permute-done.58 = bf16[24,3072]{1,0:T(8,128)(2,1)S(1)} collective-permute-done((bf16[24,3072]{1,0:T(8,128)(2,1)S(1)}, bf16[24,3072]{1,0:T(8,128)(2,1)S(1)}, u32[]{:S(2)}, u32[]{:S(2)}) %collective-permute-start.58) | collective-permute-done | bytes 147488 | tf_op jit(solution)/shard_map/ppermute | solution.py:157
  419.3 11.4 %collective-permute-done.67 = bf16[192,768]{1,0:T(8,128)(2,1)S(1)} collective-permute-done((bf16[192,768]{1,0:T(8,128)(2,1)S(1)}, bf16[192,768]{1,0:T(8,128)(2,1)S(1)}, u32[]{:S(2)}, u32[]{:S(2)}) %collective-permute-start.67) | collective-permute-done | bytes 294944 | tf_op jit(solution)/shard_map/ppermute | solution.py:157
  430.7 8.0 %collective-permute-done.59 = bf16[24,3072]{1,0:T(8,128)(2,1)S(1)} collective-permute-done((bf16[24,3072]{1,0:T(8,128)(2,1)S(1)}, bf16[24,3072]{1,0:T(8,128)(2,1)S(1)}, u32[]{:S(2)}, u32[]{:S(2)}) %collective-permute-start.59) | collective-permute-done | bytes 147488 | tf_op jit(solution)/shard_map/ppermute | solution.py:157
  438.8 3.0 collective-permute-start.60
  441.9 4.0 collective-permute-done.68
  446.1 3.2 collective-permute-done.60
  451.3 5.6 collective-permute-done.69
  459.6 5.5 collective-permute-done.70
  469.4 2.8 fusion.25
  472.1 15.5 %collective-permute-done.71 = bf16[384,768]{1,0:T(8,128)(2,1)S(1)} collective-permute-done((bf16[384,768]{1,0:T(8,128)(2,1)S(1)}, bf16[384,768]{1,0:T(8,128)(2,1)S(1)}, u32[]{:S(2)}, u32[]{:S(2)}) %collective-permute-start.71) | collective-permute-done | bytes 589856 | tf_op jit(solution)/shard_map/ppermute | solution.py:157
  488.9 17.6 %collective-permute-done.62 = bf16[192,3072]{1,0:T(8,128)(2,1)S(1)} collective-permute-done((bf16[192,3072]{1,0:T(8,128)(2,1)S(1)}, bf16[192,3072]{1,0:T(8,128)(2,1)S(1)}, u32[]{:S(2)}, u32[]{:S(2)}) %collective-permute-start.62) | collective-permute-done | bytes 1179680 | tf_op jit(solution)/shard_map/ppermute | solution.py:157
  507.6 3.2 fusion.80
  514.0 4.1 collective-permute-done.12
  532.0 3.2 collective-permute-start.16
  535.2 3.2 maximum_convert_fusion
  542.8 6.2 %fusion.7 = f32[768,3072]{1,0:T(8,128)} fusion(bf16[384,3072]{1,0:T(8,128)(2,1)} %collective-permute-done.63, bf16[384,3072]{1,0:T(8,128)(2,1)S(1)} %maximum_select_fusion.2, pred[]{:T(512)S(6)} %eq.112), kind=kLoop, calls=%fused_computation.12 | loop fusion | flops 23592960 | bytes 14155777 | tf_op jit(solution)/shard_map/convert_element_type | solution.py:350
  549.0 8.7 %fusion.8 = f32[3072,768]{1,0:T(8,128)} fusion(bf16[1536,768]{1,0:T(8,128)(2,1)} %collective-permute-done.73, bf16[1536,768]{1,0:T(8,128)(2,1)} %maximum_select_fusion.3, pred[]{:T(512)S(6)} %eq.112), kind=kLoop, calls=%fused_computation.14 | loop fusion | flops 23592960 | bytes 14155777 | tf_op jit(solution)/shard_map/convert_element_type | solution.py:350
  (382 shorter events, 129.9 us)
Async XLA Ops:
  44.3 26.0 %collective-permute-start = (bf16[3,384,768]{2,1,0:T(8,128)(2,1)}, bf16[3,384,768]{2,1,0:T(8,128)(2,1)}, u32[]{:S(2)}, u32[]{:S(2)}) collective-permute-start(bf16[3,384,768]{2,1,0:T(8,128)(2,1)} %bitcast.4), channel_id=1, source_target_pairs={{0,8},{8,0},{16,24},{24,16},{1,9},{9,1},{17,25},{25,17},{2,10},{10... | collective-permute-start | bytes 5308424 | tf_op jit(solution)/shard_map/ppermute | solution.py:157
  44.8 234.3 %collective-permute-start.17 = (bf16[768,768]{0,1:T(8,128)(2,1)}, bf16[768,768]{0,1:T(8,128)(2,1)}, u32[]{:S(2)}, u32[]{:S(2)}) collective-permute-start(bf16[768,768]{0,1:T(8,128)(2,1)} %fusion.20), channel_id=1, source_target_pairs={{0,8},{8,0},{16,24},{24,16},{1,9},{9,1},{17,25},{25,17},{2,10},{10... | collective-permute-start | bytes 3538952 | tf_op jit(solution)/shard_map/ppermute | solution.py:157
  72.4 17.9 %collective-permute-start.1 = (bf16[2,192,768]{2,1,0:T(8,128)(2,1)S(1)}, bf16[2,192,768]{2,1,0:T(8,128)(2,1)S(1)}, u32[]{:S(2)}, u32[]{:S(2)}) collective-permute-start(bf16[2,192,768]{2,1,0:T(8,128)(2,1)S(1)} %maximum_bitcast_fusion.1), channel_id=1, source_target_pairs={{16,0},{24,8},{17,1},{25,9},{18,2},{26,10},{19,3},{27,11},{20,4},{... | collective-permute-start | bytes 1769480 | tf_op jit(solution)/shard_map/ppermute | solution.py:221
  73.7 30.3 %collective-permute-start.2 = (bf16[2,2,192,768]{3,2,0,1:T(8,128)(2,1)S(1)}, bf16[2,2,192,768]{3,2,0,1:T(8,128)(2,1)S(1)}, u32[]{:S(2)}, u32[]{:S(2)}) collective-permute-start(bf16[2,2,192,768]{3,2,0,1:T(8,128)(2,1)S(1)} %pad_maximum_fusion.4), channel_id=1, source_target_pairs={{0,16},{8,24},{1,17},{9,25},{2,18},{10,26},{3,19},{11,27},{4,20},{... | collective-permute-start | bytes 3538952 | tf_op jit(solution)/shard_map/ppermute | solution.py:220
  112.6 17.0 %collective-permute-start.4 = (bf16[2,192,768]{2,1,0:T(8,128)(2,1)S(1)}, bf16[2,192,768]{2,1,0:T(8,128)(2,1)S(1)}, u32[]{:S(2)}, u32[]{:S(2)}) collective-permute-start(bf16[2,192,768]{2,1,0:T(8,128)(2,1)S(1)} %convert_element_type.275), channel_id=1, source_target_pairs={{0,16},{8,24},{1,17},{9,25},{2,18},{10,26},{3,19},{11,27},{4,20},{... | collective-permute-start | bytes 1769480 | tf_op jit(solution)/shard_map/ppermute | solution.py:227
  117.1 12.3 %collective-permute-start.3 = (f32[3,2,768]{2,1,0:T(2,128)S(1)}, f32[3,2,768]{2,1,0:T(2,128)S(1)}, u32[]{:S(2)}, u32[]{:S(2)}) collective-permute-start(f32[3,2,768]{2,1,0:T(2,128)S(1)} %get-tuple-element.21), channel_id=1, source_target_pairs={{0,16},{8,24},{1,17},{9,25},{2,18},{10,26},{3,19},{11,27},{4,20},{... | collective-permute-start | bytes 55304 | tf_op jit(solution)/shard_map/ppermute | solution.py:228
  169.6 16.5 %collective-permute-start.6 = (bf16[768,768]{0,1:T(8,128)(2,1)}, bf16[768,768]{0,1:T(8,128)(2,1)}, u32[]{:S(2)}, u32[]{:S(2)}) collective-permute-start(bf16[768,768]{0,1:T(8,128)(2,1)} %fusion.79), channel_id=1, source_target_pairs={{0,8},{8,0},{16,24},{24,16},{1,9},{9,1},{17,25},{25,17},{2,10},{10... | collective-permute-start | bytes 3538952 | tf_op jit(solution)/shard_map/ppermute | solution.py:157
  176.3 107.9 %collective-permute-start.54 = (bf16[384,3072]{1,0:T(8,128)(2,1)}, bf16[384,3072]{1,0:T(8,128)(2,1)S(1)}, u32[]{:S(2)}, u32[]{:S(2)}) collective-permute-start(bf16[384,3072]{1,0:T(8,128)(2,1)} %convolution_convert_fusion.1), channel_id=1, source_target_pairs={{0,8},{8,0},{16,24},{24,16},{1,9},{9,1},{17,25},{25,17},{2,10},{10... | collective-permute-start | bytes 7077896 | tf_op jit(solution)/shard_map/ppermute | solution.py:157
  182.1 139.0 %collective-permute-start.64 = (bf16[1536,768]{1,0:T(8,128)(2,1)}, bf16[1536,768]{1,0:T(8,128)(2,1)S(1)}, u32[]{:S(2)}, u32[]{:S(2)}) collective-permute-start(bf16[1536,768]{1,0:T(8,128)(2,1)} %convolution_convert_fusion.2), channel_id=1, source_target_pairs={{0,8},{8,0},{16,24},{24,16},{1,9},{9,1},{17,25},{25,17},{2,10},{10... | collective-permute-start | bytes 7077896 | tf_op jit(solution)/shard_map/ppermute | solution.py:157
  188.2 13.4 %collective-permute-start.45 = (bf16[192,768]{1,0:T(8,128)(2,1)S(1)}, bf16[192,768]{1,0:T(8,128)(2,1)S(1)}, u32[]{:S(2)}, u32[]{:S(2)}) collective-permute-start(bf16[192,768]{1,0:T(8,128)(2,1)S(1)} %dynamic-slice_convert_fusion.6), channel_id=1, source_target_pairs={{0,2},{1,3},{2,0},{3,1},{4,6},{5,7},{6,4},{7,5},{8,10},{9,11},{10,... | collective-permute-start | bytes 884744 | tf_op jit(solution)/shard_map/ppermute | solution.py:157
  196.7 33.5 %collective-permute-start.7 = (bf16[2,192,768]{2,1,0:T(8,128)(2,1)S(1)}, bf16[2,192,768]{2,1,0:T(8,128)(2,1)S(1)}, u32[]{:S(2)}, u32[]{:S(2)}) collective-permute-start(bf16[2,192,768]{2,1,0:T(8,128)(2,1)S(1)} %fusion.53), channel_id=1, source_target_pairs={{16,0},{24,8},{17,1},{25,9},{18,2},{26,10},{19,3},{27,11},{20,4},{... | collective-permute-start | bytes 1769480 | tf_op jit(solution)/shard_map/ppermute | solution.py:286
  201.7 9.7 %collective-permute-start.46 = (bf16[96,768]{1,0:T(8,128)(2,1)S(1)}, bf16[96,768]{1,0:T(8,128)(2,1)S(1)}, u32[]{:S(2)}, u32[]{:S(2)}) collective-permute-start(bf16[96,768]{1,0:T(8,128)(2,1)S(1)} %dynamic-slice_convert_fusion.12), channel_id=1, source_target_pairs={{0,4},{1,5},{2,6},{3,7},{4,0},{5,1},{6,2},{7,3},{8,12},{9,13},{10,... | collective-permute-start | bytes 442376 | tf_op jit(solution)/shard_map/ppermute | solution.py:157
  211.4 4.9 collective-permute-start.47
  220.3 5.8 %collective-permute-start.8 = (f32[2,3,2,768]{3,2,1,0:T(2,128)S(1)}, f32[2,3,2,768]{3,2,1,0:T(2,128)S(1)}, u32[]{:S(2)}, u32[]{:S(2)}) collective-permute-start(f32[2,3,2,768]{3,2,1,0:T(2,128)S(1)} %pad_maximum_fusion.6), channel_id=1, source_target_pairs={{16,0},{24,8},{17,1},{25,9},{18,2},{26,10},{19,3},{27,11},{20,4},{... | collective-permute-start | bytes 110600 | tf_op jit(solution)/shard_map/ppermute | solution.py:287
  234.6 15.2 %collective-permute-start.51 = (bf16[96,768]{1,0:T(8,128)(2,1)S(1)}, bf16[96,768]{1,0:T(8,128)(2,1)S(1)}, u32[]{:S(2)}, u32[]{:S(2)}) collective-permute-start(bf16[96,768]{1,0:T(8,128)(2,1)S(1)} %maximum_select_fusion.28), channel_id=1, source_target_pairs={{0,4},{1,5},{2,6},{3,7},{4,0},{5,1},{6,2},{7,3},{8,12},{9,13},{10,... | collective-permute-start | bytes 442376 | tf_op jit(solution)/shard_map/ppermute | solution.py:157
  247.8 29.2 %collective-permute-start.9 = (bf16[2,192,768]{2,1,0:T(8,128)(2,1)S(1)}, bf16[2,192,768]{2,1,0:T(8,128)(2,1)S(1)}, u32[]{:S(2)}, u32[]{:S(2)}) collective-permute-start(bf16[2,192,768]{2,1,0:T(8,128)(2,1)S(1)} %get-tuple-element.24), channel_id=1, source_target_pairs={{0,16},{8,24},{1,17},{9,25},{2,18},{10,26},{3,19},{11,27},{4,20},{... | collective-permute-start | bytes 1769480 | tf_op jit(solution)/shard_map/ppermute | solution.py:302
  249.8 25.5 %collective-permute-start.52 = (bf16[192,768]{1,0:T(8,128)(2,1)S(1)}, bf16[192,768]{1,0:T(8,128)(2,1)S(1)}, u32[]{:S(2)}, u32[]{:S(2)}) collective-permute-start(bf16[192,768]{1,0:T(8,128)(2,1)S(1)} %maximum_select_fusion.22), channel_id=1, source_target_pairs={{0,2},{1,3},{2,0},{3,1},{4,6},{5,7},{6,4},{7,5},{8,10},{9,11},{10,... | collective-permute-start | bytes 884744 | tf_op jit(solution)/shard_map/ppermute | solution.py:157
  275.3 55.1 %collective-permute-start.10 = (bf16[2,2,192,768]{3,2,1,0:T(8,128)(2,1)S(1)}, bf16[2,2,192,768]{3,2,1,0:T(8,128)(2,1)S(1)}, u32[]{:S(2)}, u32[]{:S(2)}) collective-permute-start(bf16[2,2,192,768]{3,2,1,0:T(8,128)(2,1)S(1)} %pad_maximum_fusion.5), channel_id=1, source_target_pairs={{16,0},{24,8},{17,1},{25,9},{18,2},{26,10},{19,3},{27,11},{20,4},{... | collective-permute-start | bytes 3538952 | tf_op jit(solution)/shard_map/ppermute | solution.py:303
  281.4 24.6 %collective-permute-start.18 = (bf16[384,384]{1,0:T(8,128)(2,1)S(1)}, bf16[384,384]{1,0:T(8,128)(2,1)S(1)}, u32[]{:S(2)}, u32[]{:S(2)}) collective-permute-start(bf16[384,384]{1,0:T(8,128)(2,1)S(1)} %dynamic-slice_convert_fusion.9), channel_id=1, source_target_pairs={{0,16},{8,24},{16,0},{24,8},{1,17},{9,25},{17,1},{25,9},{2,18},{10... | collective-permute-start | bytes 884744 | tf_op jit(solution)/shard_map/ppermute | solution.py:157
  306.1 11.1 %collective-permute-start.19 = (bf16[192,384]{1,0:T(8,128)(2,1)S(1)}, bf16[192,384]{1,0:T(8,128)(2,1)S(1)}, u32[]{:S(2)}, u32[]{:S(2)}) collective-permute-start(bf16[192,384]{1,0:T(8,128)(2,1)S(1)} %dynamic-slice_convert_fusion.15), channel_id=1, source_target_pairs={{0,1},{1,0},{2,3},{3,2},{4,5},{5,4},{6,7},{7,6},{8,9},{9,8},{10,11... | collective-permute-start | bytes 442376 | tf_op jit(solution)/shard_map/ppermute | solution.py:157
  312.5 68.8 %collective-permute-start.55 = (bf16[192,3072]{1,0:T(8,128)(2,1)S(1)}, bf16[192,3072]{1,0:T(8,128)(2,1)S(1)}, u32[]{:S(2)}, u32[]{:S(2)}) collective-permute-start(bf16[192,3072]{1,0:T(8,128)(2,1)S(1)} %dynamic-slice_convert_fusion.1), channel_id=1, source_target_pairs={{0,1},{1,0},{2,3},{3,2},{4,5},{5,4},{6,7},{7,6},{8,9},{9,8},{10,11... | collective-permute-start | bytes 3538952 | tf_op jit(solution)/shard_map/ppermute | solution.py:157
  317.2 7.7 %collective-permute-start.20 = (bf16[96,384]{1,0:T(8,128)(2,1)S(1)}, bf16[96,384]{1,0:T(8,128)(2,1)S(1)}, u32[]{:S(2)}, u32[]{:S(2)}) collective-permute-start(bf16[96,384]{1,0:T(8,128)(2,1)S(1)} %dynamic-slice_convert_fusion.19), channel_id=1, source_target_pairs={{0,2},{1,3},{2,0},{3,1},{4,6},{5,7},{6,4},{7,5},{8,10},{9,11},{10,... | collective-permute-start | bytes 221192 | tf_op jit(solution)/shard_map/ppermute | solution.py:157
  325.0 5.3 collective-permute-start.21
  325.5 59.2 %collective-permute-start.65 = (bf16[768,768]{1,0:T(8,128)(2,1)S(1)}, bf16[768,768]{1,0:T(8,128)(2,1)S(1)}, u32[]{:S(2)}, u32[]{:S(2)}) collective-permute-start(bf16[768,768]{1,0:T(8,128)(2,1)S(1)} %dynamic-slice_convert_fusion), channel_id=1, source_target_pairs={{0,16},{8,24},{16,0},{24,8},{1,17},{9,25},{17,1},{25,9},{2,18},{10... | collective-permute-start | bytes 3538952 | tf_op jit(solution)/shard_map/ppermute | solution.py:157
  330.3 5.0 collective-permute-start.22
  333.7 135.2 %collective-permute-start.11 = (bf16[3,384,768]{2,1,0:T(8,128)(2,1)S(1)}, bf16[3,384,768]{2,1,0:T(8,128)(2,1)S(1)}, u32[]{:S(2)}, u32[]{:S(2)}) collective-permute-start(bf16[3,384,768]{2,1,0:T(8,128)(2,1)S(1)} %get-tuple-element.79), channel_id=1, source_target_pairs={{0,8},{8,0},{16,24},{24,16},{1,9},{9,1},{17,25},{25,17},{2,10},{10... | collective-permute-start | bytes 5308424 | tf_op jit(solution)/shard_map/ppermute | solution.py:157
  335.3 6.2 %collective-permute-start.23 = (bf16[96,384]{1,0:T(8,128)(2,1)S(1)}, bf16[96,384]{1,0:T(8,128)(2,1)S(1)}, u32[]{:S(2)}, u32[]{:S(2)}) collective-permute-start(bf16[96,384]{1,0:T(8,128)(2,1)S(1)} %maximum_select_fusion.29), channel_id=1, source_target_pairs={{0,2},{1,3},{2,0},{3,1},{4,6},{5,7},{6,4},{7,5},{8,10},{9,11},{10,... | collective-permute-start | bytes 221192 | tf_op jit(solution)/shard_map/ppermute | solution.py:157
  339.5 8.0 %collective-permute-start.36 = (bf16[384,384]{1,0:T(8,128)(2,1)S(1)}, bf16[384,384]{1,0:T(8,128)(2,1)S(1)}, u32[]{:S(2)}, u32[]{:S(2)}) collective-permute-start(bf16[384,384]{1,0:T(8,128)(2,1)S(1)} %dynamic-slice_convert_fusion.7), channel_id=1, source_target_pairs={{0,2},{1,3},{2,0},{3,1},{4,6},{5,7},{6,4},{7,5},{8,10},{9,11},{10,... | collective-permute-start | bytes 884744 | tf_op jit(solution)/shard_map/ppermute | solution.py:157
  341.5 5.2 collective-permute-start.24
  346.7 6.7 %collective-permute-start.27 = (bf16[384,384]{1,0:T(8,128)(2,1)S(1)}, bf16[384,384]{1,0:T(8,128)(2,1)S(1)}, u32[]{:S(2)}, u32[]{:S(2)}) collective-permute-start(bf16[384,384]{1,0:T(8,128)(2,1)S(1)} %dynamic-slice_convert_fusion.8), channel_id=1, source_target_pairs={{0,1},{1,0},{2,3},{3,2},{4,5},{5,4},{6,7},{7,6},{8,9},{9,8},{10,11... | collective-permute-start | bytes 884744 | tf_op jit(solution)/shard_map/ppermute | solution.py:157
  347.6 110.7 %collective-permute-start.25 = (bf16[384,384]{1,0:T(8,128)(2,1)S(1)}, bf16[384,384]{1,0:T(8,128)(2,1)S(1)}, u32[]{:S(2)}, u32[]{:S(2)}) collective-permute-start(bf16[384,384]{1,0:T(8,128)(2,1)S(1)} %maximum_select_fusion.19), channel_id=1, source_target_pairs={{0,16},{8,24},{16,0},{24,8},{1,17},{9,25},{17,1},{25,9},{2,18},{10... | collective-permute-start | bytes 884744 | tf_op jit(solution)/shard_map/ppermute | solution.py:157
  353.4 7.9 %collective-permute-start.37 = (bf16[192,384]{1,0:T(8,128)(2,1)S(1)}, bf16[192,384]{1,0:T(8,128)(2,1)S(1)}, u32[]{:S(2)}, u32[]{:S(2)}) collective-permute-start(bf16[192,384]{1,0:T(8,128)(2,1)S(1)} %dynamic-slice_convert_fusion.13), channel_id=1, source_target_pairs={{0,4},{1,5},{2,6},{3,7},{4,0},{5,1},{6,2},{7,3},{8,12},{9,13},{10,... | collective-permute-start | bytes 442376 | tf_op jit(solution)/shard_map/ppermute | solution.py:157
  361.4 5.5 collective-permute-start.28
  379.6 4.9 collective-permute-start.30
  381.4 5.3 collective-permute-start.40
  384.5 10.7 %collective-permute-start.56 = (bf16[96,3072]{1,0:T(8,128)(2,1)S(1)}, bf16[96,3072]{1,0:T(8,128)(2,1)S(1)}, u32[]{:S(2)}, u32[]{:S(2)}) collective-permute-start(bf16[96,3072]{1,0:T(8,128)(2,1)S(1)} %dynamic-slice_convert_fusion.3), channel_id=1, source_target_pairs={{0,16},{8,24},{16,0},{24,8},{1,17},{9,25},{17,1},{25,9},{2,18},{10... | collective-permute-start | bytes 1769480 | tf_op jit(solution)/shard_map/ppermute | solution.py:157
  384.7 10.8 %collective-permute-start.31 = (bf16[48,384]{1,0:T(8,128)(2,1)S(1)}, bf16[48,384]{1,0:T(8,128)(2,1)S(1)}, u32[]{:S(2)}, u32[]{:S(2)}) collective-permute-start(bf16[48,384]{1,0:T(8,128)(2,1)S(1)} %add_convert_fusion.8), channel_id=1, source_target_pairs={{0,4},{1,5},{2,6},{3,7},{4,0},{5,1},{6,2},{7,3},{8,12},{9,13},{10,... | collective-permute-start | bytes 110600 | tf_op jit(solution)/shard_map/ppermute | solution.py:157
  386.7 21.9 %collective-permute-start.66 = (bf16[384,768]{1,0:T(8,128)(2,1)S(1)}, bf16[384,768]{1,0:T(8,128)(2,1)S(1)}, u32[]{:S(2)}, u32[]{:S(2)}) collective-permute-start(bf16[384,768]{1,0:T(8,128)(2,1)S(1)} %dynamic-slice_convert_fusion.2), channel_id=1, source_target_pairs={{0,1},{1,0},{2,3},{3,2},{4,5},{5,4},{6,7},{7,6},{8,9},{9,8},{10,11... | collective-permute-start | bytes 1769480 | tf_op jit(solution)/shard_map/ppermute | solution.py:157
  395.2 4.6 collective-permute-start.41
  395.6 10.7 %collective-permute-start.57 = (bf16[48,3072]{1,0:T(8,128)(2,1)S(1)}, bf16[48,3072]{1,0:T(8,128)(2,1)S(1)}, u32[]{:S(2)}, u32[]{:S(2)}) collective-permute-start(bf16[48,3072]{1,0:T(8,128)(2,1)S(1)} %dynamic-slice_convert_fusion.5), channel_id=1, source_target_pairs={{0,2},{1,3},{2,0},{3,1},{4,6},{5,7},{6,4},{7,5},{8,10},{9,11},{10,... | collective-permute-start | bytes 884744 | tf_op jit(solution)/shard_map/ppermute | solution.py:157
  399.7 6.5 %collective-permute-start.32 = (bf16[96,384]{1,0:T(8,128)(2,1)S(1)}, bf16[96,384]{1,0:T(8,128)(2,1)S(1)}, u32[]{:S(2)}, u32[]{:S(2)}) collective-permute-start(bf16[96,384]{1,0:T(8,128)(2,1)S(1)} %maximum_select_fusion.30), channel_id=1, source_target_pairs={{0,2},{1,3},{2,0},{3,1},{4,6},{5,7},{6,4},{7,5},{8,10},{9,11},{10,... | collective-permute-start | bytes 221192 | tf_op jit(solution)/shard_map/ppermute | solution.py:157
  406.2 32.6 %collective-permute-start.42 = (bf16[192,384]{1,0:T(8,128)(2,1)S(1)}, bf16[192,384]{1,0:T(8,128)(2,1)S(1)}, u32[]{:S(2)}, u32[]{:S(2)}) collective-permute-start(bf16[192,384]{1,0:T(8,128)(2,1)S(1)} %maximum_select_fusion.27), channel_id=1, source_target_pairs={{0,4},{1,5},{2,6},{3,7},{4,0},{5,1},{6,2},{7,3},{8,12},{9,13},{10,... | collective-permute-start | bytes 442376 | tf_op jit(solution)/shard_map/ppermute | solution.py:157
  406.3 52.3 %collective-permute-start.33 = (bf16[192,384]{1,0:T(8,128)(2,1)S(1)}, bf16[192,384]{1,0:T(8,128)(2,1)S(1)}, u32[]{:S(2)}, u32[]{:S(2)}) collective-permute-start(bf16[192,384]{1,0:T(8,128)(2,1)S(1)} %maximum_select_fusion.26), channel_id=1, source_target_pairs={{0,16},{8,24},{16,0},{24,8},{1,17},{9,25},{17,1},{25,9},{2,18},{10... | collective-permute-start | bytes 442376 | tf_op jit(solution)/shard_map/ppermute | solution.py:157
  408.6 10.6 %collective-permute-start.58 = (bf16[24,3072]{1,0:T(8,128)(2,1)S(1)}, bf16[24,3072]{1,0:T(8,128)(2,1)S(1)}, u32[]{:S(2)}, u32[]{:S(2)}) collective-permute-start(bf16[24,3072]{1,0:T(8,128)(2,1)S(1)} %dynamic-slice_convert_fusion.11), channel_id=1, source_target_pairs={{0,4},{1,5},{2,6},{3,7},{4,0},{5,1},{6,2},{7,3},{8,12},{9,13},{10,... | collective-permute-start | bytes 442376 | tf_op jit(solution)/shard_map/ppermute | solution.py:157
  419.2 11.4 %collective-permute-start.67 = (bf16[192,768]{1,0:T(8,128)(2,1)S(1)}, bf16[192,768]{1,0:T(8,128)(2,1)S(1)}, u32[]{:S(2)}, u32[]{:S(2)}) collective-permute-start(bf16[192,768]{1,0:T(8,128)(2,1)S(1)} %dynamic-slice_convert_fusion.4), channel_id=1, source_target_pairs={{0,2},{1,3},{2,0},{3,1},{4,6},{5,7},{6,4},{7,5},{8,10},{9,11},{10,... | collective-permute-start | bytes 884744 | tf_op jit(solution)/shard_map/ppermute | solution.py:157
  430.6 8.1 %collective-permute-start.59 = (bf16[24,3072]{1,0:T(8,128)(2,1)S(1)}, bf16[24,3072]{1,0:T(8,128)(2,1)S(1)}, u32[]{:S(2)}, u32[]{:S(2)}) collective-permute-start(bf16[24,3072]{1,0:T(8,128)(2,1)S(1)} %add_convert_fusion.5), channel_id=1, source_target_pairs={{0,4},{1,5},{2,6},{3,7},{4,0},{5,1},{6,2},{7,3},{8,12},{9,13},{10,... | collective-permute-start | bytes 442376 | tf_op jit(solution)/shard_map/ppermute | solution.py:157
  438.8 7.2 %collective-permute-start.68 = (bf16[96,768]{1,0:T(8,128)(2,1)S(1)}, bf16[96,768]{1,0:T(8,128)(2,1)S(1)}, u32[]{:S(2)}, u32[]{:S(2)}) collective-permute-start(bf16[96,768]{1,0:T(8,128)(2,1)S(1)} %dynamic-slice_convert_fusion.10), channel_id=1, source_target_pairs={{0,4},{1,5},{2,6},{3,7},{4,0},{5,1},{6,2},{7,3},{8,12},{9,13},{10,... | collective-permute-start | bytes 442376 | tf_op jit(solution)/shard_map/ppermute | solution.py:157
  438.8 10.4 %collective-permute-start.60 = (bf16[48,3072]{1,0:T(8,128)(2,1)S(1)}, bf16[48,3072]{1,0:T(8,128)(2,1)S(1)}, u32[]{:S(2)}, u32[]{:S(2)}) collective-permute-start(bf16[48,3072]{1,0:T(8,128)(2,1)S(1)} %maximum_select_fusion.23), channel_id=1, source_target_pairs={{0,2},{1,3},{2,0},{3,1},{4,6},{5,7},{6,4},{7,5},{8,10},{9,11},{10,... | collective-permute-start | bytes 884744 | tf_op jit(solution)/shard_map/ppermute | solution.py:157
  446.0 12.9 %collective-permute-start.43 = (bf16[384,384]{1,0:T(8,128)(2,1)S(1)}, bf16[384,384]{1,0:T(8,128)(2,1)S(1)}, u32[]{:S(2)}, u32[]{:S(2)}) collective-permute-start(bf16[384,384]{1,0:T(8,128)(2,1)S(1)} %maximum_select_fusion.21), channel_id=1, source_target_pairs={{0,2},{1,3},{2,0},{3,1},{4,6},{5,7},{6,4},{7,5},{8,10},{9,11},{10,... | collective-permute-start | bytes 884744 | tf_op jit(solution)/shard_map/ppermute | solution.py:157
  449.2 7.6 %collective-permute-start.69 = (bf16[96,768]{1,0:T(8,128)(2,1)S(1)}, bf16[96,768]{1,0:T(8,128)(2,1)S(1)}, u32[]{:S(2)}, u32[]{:S(2)}) collective-permute-start(bf16[96,768]{1,0:T(8,128)(2,1)S(1)} %add_convert_fusion.4), channel_id=1, source_target_pairs={{0,4},{1,5},{2,6},{3,7},{4,0},{5,1},{6,2},{7,3},{8,12},{9,13},{10,... | collective-permute-start | bytes 442376 | tf_op jit(solution)/shard_map/ppermute | solution.py:157
  456.8 10.1 %collective-permute-start.61 = (bf16[96,3072]{1,0:T(8,128)(2,1)S(1)}, bf16[96,3072]{1,0:T(8,128)(2,1)S(1)}, u32[]{:S(2)}, u32[]{:S(2)}) collective-permute-start(bf16[96,3072]{1,0:T(8,128)(2,1)S(1)} %maximum_select_fusion.17), channel_id=1, source_target_pairs={{0,16},{8,24},{16,0},{24,8},{1,17},{9,25},{17,1},{25,9},{2,18},{10... | collective-permute-start | bytes 1769480 | tf_op jit(solution)/shard_map/ppermute | solution.py:157
  458.3 6.8 %collective-permute-start.70 = (bf16[192,768]{1,0:T(8,128)(2,1)S(1)}, bf16[192,768]{1,0:T(8,128)(2,1)S(1)}, u32[]{:S(2)}, u32[]{:S(2)}) collective-permute-start(bf16[192,768]{1,0:T(8,128)(2,1)S(1)} %maximum_select_fusion.24), channel_id=1, source_target_pairs={{0,2},{1,3},{2,0},{3,1},{4,6},{5,7},{6,4},{7,5},{8,10},{9,11},{10,... | collective-permute-start | bytes 884744 | tf_op jit(solution)/shard_map/ppermute | solution.py:157
  458.6 54.6 %collective-permute-start.53 = (bf16[384,768]{1,0:T(8,128)(2,1)S(1)}, bf16[384,768]{1,0:T(8,128)(2,1)S(1)}, u32[]{:S(2)}, u32[]{:S(2)}) collective-permute-start(bf16[384,768]{1,0:T(8,128)(2,1)S(1)} %maximum_select_fusion.16), channel_id=1, source_target_pairs={{0,8},{8,0},{16,24},{24,16},{1,9},{9,1},{17,25},{25,17},{2,10},{10... | collective-permute-start | bytes 1769480 | tf_op jit(solution)/shard_map/ppermute | solution.py:157
  458.8 61.0 %collective-permute-start.26 = (bf16[768,384]{1,0:T(8,128)(2,1)S(1)}, bf16[768,384]{1,0:T(8,128)(2,1)S(1)}, u32[]{:S(2)}, u32[]{:S(2)}) collective-permute-start(bf16[768,384]{1,0:T(8,128)(2,1)S(1)} %maximum_select_fusion.13), channel_id=1, source_target_pairs={{0,8},{8,0},{16,24},{24,16},{1,9},{9,1},{17,25},{25,17},{2,10},{10... | collective-permute-start | bytes 1769480 | tf_op jit(solution)/shard_map/ppermute | solution.py:157
  465.1 48.2 %collective-permute-start.34 = (bf16[384,384]{1,0:T(8,128)(2,1)S(1)}, bf16[384,384]{1,0:T(8,128)(2,1)S(1)}, u32[]{:S(2)}, u32[]{:S(2)}) collective-permute-start(bf16[384,384]{1,0:T(8,128)(2,1)S(1)} %maximum_select_fusion.20), channel_id=1, source_target_pairs={{0,1},{1,0},{2,3},{3,2},{4,5},{5,4},{6,7},{7,6},{8,9},{9,8},{10,11... | collective-permute-start | bytes 884744 | tf_op jit(solution)/shard_map/ppermute | solution.py:157
  466.9 20.8 %collective-permute-start.71 = (bf16[384,768]{1,0:T(8,128)(2,1)S(1)}, bf16[384,768]{1,0:T(8,128)(2,1)S(1)}, u32[]{:S(2)}, u32[]{:S(2)}) collective-permute-start(bf16[384,768]{1,0:T(8,128)(2,1)S(1)} %maximum_select_fusion.18), channel_id=1, source_target_pairs={{0,1},{1,0},{2,3},{3,2},{4,5},{5,4},{6,7},{7,6},{8,9},{9,8},{10,11... | collective-permute-start | bytes 1769480 | tf_op jit(solution)/shard_map/ppermute | solution.py:157
  468.9 37.6 %collective-permute-start.62 = (bf16[192,3072]{1,0:T(8,128)(2,1)S(1)}, bf16[192,3072]{1,0:T(8,128)(2,1)S(1)}, u32[]{:S(2)}, u32[]{:S(2)}) collective-permute-start(bf16[192,3072]{1,0:T(8,128)(2,1)S(1)} %maximum_select_fusion.11), channel_id=1, source_target_pairs={{0,1},{1,0},{2,3},{3,2},{4,5},{5,4},{6,7},{7,6},{8,9},{9,8},{10,11... | collective-permute-start | bytes 3538952 | tf_op jit(solution)/shard_map/ppermute | solution.py:157
  488.2 22.7 %collective-permute-start.72 = (bf16[768,768]{1,0:T(8,128)(2,1)S(1)}, bf16[768,768]{1,0:T(8,128)(2,1)S(1)}, u32[]{:S(2)}, u32[]{:S(2)}) collective-permute-start(bf16[768,768]{1,0:T(8,128)(2,1)S(1)} %maximum_select_fusion.12), channel_id=1, source_target_pairs={{0,16},{8,24},{16,0},{24,8},{1,17},{9,25},{17,1},{25,9},{2,18},{10... | collective-permute-start | bytes 3538952 | tf_op jit(solution)/shard_map/ppermute | solution.py:157
  507.4 35.3 %collective-permute-start.63 = (bf16[384,3072]{1,0:T(8,128)(2,1)S(1)}, bf16[384,3072]{1,0:T(8,128)(2,1)}, u32[]{:S(2)}, u32[]{:S(2)}) collective-permute-start(bf16[384,3072]{1,0:T(8,128)(2,1)S(1)} %maximum_select_fusion.2), channel_id=1, source_target_pairs={{0,8},{8,0},{16,24},{24,16},{1,9},{9,1},{17,25},{25,17},{2,10},{10... | collective-permute-start | bytes 7077896 | tf_op jit(solution)/shard_map/ppermute | solution.py:157
  512.6 36.4 %collective-permute-start.73 = (bf16[1536,768]{1,0:T(8,128)(2,1)}, bf16[1536,768]{1,0:T(8,128)(2,1)}, u32[]{:S(2)}, u32[]{:S(2)}) collective-permute-start(bf16[1536,768]{1,0:T(8,128)(2,1)} %maximum_select_fusion.3), channel_id=1, source_target_pairs={{0,8},{8,0},{16,24},{24,16},{1,9},{9,1},{17,25},{25,17},{2,10},{10... | collective-permute-start | bytes 7077896 | tf_op jit(solution)/shard_map/ppermute | solution.py:157
  513.2 12.2 %collective-permute-start.44 = (bf16[768,384]{1,0:T(8,128)(2,1)S(1)}, bf16[768,384]{1,0:T(8,128)(2,1)S(1)}, u32[]{:S(2)}, u32[]{:S(2)}) collective-permute-start(bf16[768,384]{1,0:T(8,128)(2,1)S(1)} %maximum_select_fusion.15), channel_id=1, source_target_pairs={{0,8},{8,0},{16,24},{24,16},{1,9},{9,1},{17,25},{25,17},{2,10},{10... | collective-permute-start | bytes 1769480 | tf_op jit(solution)/shard_map/ppermute | solution.py:157
  513.3 4.7 collective-permute-start.12
  518.0 11.6 %collective-permute-start.35 = (bf16[768,384]{1,0:T(8,128)(2,1)S(1)}, bf16[768,384]{1,0:T(8,128)(2,1)S(1)}, u32[]{:S(2)}, u32[]{:S(2)}) collective-permute-start(bf16[768,384]{1,0:T(8,128)(2,1)S(1)} %maximum_select_fusion.14), channel_id=1, source_target_pairs={{0,8},{8,0},{16,24},{24,16},{1,9},{9,1},{17,25},{25,17},{2,10},{10... | collective-permute-start | bytes 1769480 | tf_op jit(solution)/shard_map/ppermute | solution.py:157
  532.0 8.8 %collective-permute-start.16 = (f32[6,768]{1,0:T(8,128)}, f32[6,768]{1,0:T(8,128)}, u32[]{:S(2)}, u32[]{:S(2)}) collective-permute-start(f32[6,768]{1,0:T(8,128)} %add.424), channel_id=1, source_target_pairs={{0,4},{1,5},{2,6},{3,7},{4,0},{5,1},{6,2},{7,3},{8,12},{9,13},{10,... | collective-permute-start | bytes 55304 | tf_op jit(solution)/shard_map/ppermute | solution.py:157
  (69 other events, 924.7 us)

commit v2 on v1

v2 whole, which is shorter than its diff:
```python
import functools
import math

import jax
import jax.numpy as jnp
from jax import lax
from jax.experimental import pallas as pl
from jax.experimental.pallas import tpu as pltpu
from jax.sharding import PartitionSpec as P

D = 768
HEADS = 12
HEAD_DIM = 64
SHORT = 256
FF_TILE = 512
GROUP = D // 2
HALF = GROUP // 2
HALF_HEADS = HEADS // 4
EPS = 1e-05
SCALE = HEAD_DIM**-0.5
SCALE2 = SCALE * math.log2(math.e)
BF = jnp.bfloat16
F32 = jnp.float32


def dot(a, b, ca, cb):
    return lax.dot_general(a, b, (((ca,), (cb,)), ((), ())), preferred_element_type=F32)


def cost(us):
    return pl.CostEstimate(flops=int(us * 1.1e9), bytes_accessed=1 << 20, transcendentals=0)


def params(mib):
    return pltpu.CompilerParams(vmem_limit_bytes=mib << 20)


def call(kernel, flags, grid, ins, outs, us, name, mib=48, scratch=()):
    return pl.pallas_call(
        kernel,
        grid_spec=pltpu.PrefetchScalarGridSpec(
            num_scalar_prefetch=1,
            grid=grid,
            in_specs=[pl.BlockSpec(block, index) for _, block, index in ins],
            out_specs=[pl.BlockSpec(block, index) for _, _, block, index in outs],
            scratch_shapes=list(scratch),
        ),
        out_shape=[jax.ShapeDtypeStruct(shape, dtype) for shape, dtype, _, _ in outs],
        cost_estimate=cost(us),
        compiler_params=params(mib),
        name=name,
    )(flags, *[array for array, _, _ in ins])


def fixed(array):
    return (array, array.shape, lambda i, f: (0,) * array.ndim)


def out_fixed(shape, dtype):
    return (shape, dtype, shape, lambda i, f: (0,) * len(shape))


def row(vector):
    return vector.reshape(1, -1)


def one_sequence(f):
    return f[0] == 1


def hidden_of(x_ref, emb_ref):
    return x_ref[...].astype(F32) + emb_ref[0]


def centered(values):
    center = values - jnp.mean(values, axis=-1, keepdims=True)
    return center, lax.rsqrt(jnp.mean(center * center, axis=-1, keepdims=True) + EPS)


def write_part(part, out_ref, low_ref, high_ref, value):
    out_ref[...] = value

    @pl.when(part == 0)
    def _():
        high_ref[...] = value[HALF:]

    @pl.when(part > 0)
    def _():
        low_ref[pl.ds(pl.multiple_of((part - 1) * HALF, HALF), HALF), :] = value[:HALF]


def norm_project_kernel(f, x_ref, emb_ref, gain_ref, w_ref, normed_ref, out_ref, low_ref, high_ref):
    part = pl.program_id(0)

    @pl.when(part == 0)
    def _():
        center, inv = centered(hidden_of(x_ref, emb_ref))
        normed_ref[...] = (center * inv * gain_ref[...]).T.astype(BF)

    value = dot(w_ref[...], normed_ref[...], 0, 0).astype(BF)
    write_part(part, out_ref, low_ref, high_ref, value)


def project_kernel(f, normed_ref, w_ref, out_ref, low_ref, high_ref):
    value = dot(w_ref[...], normed_ref[...], 0, 0).astype(BF)
    write_part(pl.program_id(0), out_ref, low_ref, high_ref, value)


def projection_outs(length):
    return [
        ((3 * GROUP, length), BF, (GROUP, length), lambda i, f: (i, 0)),
        out_fixed((2 * HALF, length), BF),
        out_fixed((HALF, length), BF),
    ]


def mask_tail(scores):
    n = scores.shape[0]
    key = lax.broadcasted_iota(jnp.int32, (SHORT, SHORT), 0)
    query = lax.broadcasted_iota(jnp.int32, (SHORT, SHORT), 1)
    diag = jnp.where(key <= query, scores[n - SHORT :], -1e30)
    return diag if n == SHORT else jnp.concatenate([scores[: n - SHORT], diag], 0)


def sweep(f, length, tile, variants):
    for condition, units in variants:
        for whole in (True, False):

            @pl.when(condition & (one_sequence(f) == whole))
            def _():
                for at in range(length // SHORT):
                    for unit in units:
                        tile(unit, at, 0 if whole else at)


def spans(at, first):
    return slice(at * SHORT, (at + 1) * SHORT), slice(first * SHORT, (at + 1) * SHORT)


def softmax_tile(q_refs, k_refs, v_refs, o_refs, lse_ref, unit, at, first):
    qp, keys = unit
    qs, ks = spans(at, first)
    q = q_refs[qp][:, qs]
    scores = [mask_tail(dot(k_refs[kp][:, ks], q, 0, 0) * SCALE2) for kp in keys]
    top = functools.reduce(jnp.maximum, [jnp.max(s, axis=0, keepdims=True) for s in scores])
    raw = [jnp.exp2(s - top) for s in scores]
    total = functools.reduce(jnp.add, [jnp.sum(p, axis=0, keepdims=True) for p in raw])
    out = functools.reduce(
        jnp.add, [dot(v_refs[kp][:, ks], p.astype(BF), 1, 0) for kp, p in zip(keys, raw)]
    )
    o_refs[qp][:, qs] = (out * (1.0 / total)).astype(o_refs[qp].dtype)
    lse_ref[0, qp : qp + 1, qs] = top + jnp.log2(total)


LOCAL_UNITS = (
    lambda f: (f[1] == 0, [(0, [0]), (1, [0, 1])]),
    lambda f: (f[1] == 1, [(1, [1]), (0, [0, 1])]),
)
CROSS_UNITS = [(0, [0, 1]), (1, [0, 1])]


def local_kernel(f, q0, q1, k0, k1, v0, v1, o0, o1, lse_ref):
    sweep(
        f,
        q0.shape[1],
        functools.partial(softmax_tile, (q0, q1), (k0, k1), (v0, v1), (o0, o1), lse_ref),
        [unit(f) for unit in LOCAL_UNITS],
    )


def cross_kernel(f, *refs):
    ins, (o_ref, lse_ref) = refs[:12], refs[12:]
    outs = (o_ref.at[0], o_ref.at[1])
    for early, at in ((1, 0), (0, 6)):
        q0, q1, k0, k1, v0, v1 = ins[at : at + 6]
        sweep(
            f,
            q0.shape[1],
            functools.partial(softmax_tile, (q0, q1), (k0, k1), (v0, v1), outs, lse_ref),
            [(f[2] == early, CROSS_UNITS)],
        )


def head(array, at):
    return (array, (HEAD_DIM, array.shape[-1]), lambda h, f: (at + h, 0))


def lse_spec(array):
    return (array, (1,) + array.shape[1:], lambda h, f: (h, 0, 0))


def lse_out(heads, length):
    return ((heads, 2, length), F32, (1, 2, length), lambda h, f: (h, 0, 0))


def cross_inputs(early_q, own, other, late_kv):
    return [
        head(early_q[0], 0),
        head(early_q[1], 0),
        head(own, 6 + HALF_HEADS),
        head(other, 6 + HALF_HEADS),
        head(own, 12 + HALF_HEADS),
        head(other, 12 + HALF_HEADS),
        head(own, 0),
        head(other, 0),
        head(late_kv[0], 0),
        head(late_kv[1], 0),
        head(late_kv[0], HALF_HEADS),
        head(late_kv[1], HALF_HEADS),
    ]


def merge_kernel(f, o0, o1, lse_ref, oc_ref, lsec_ref, ob_ref, lseb_ref, a0, a1, lse_out_ref, high_ref, lse_high_ref):
    half = pl.program_id(0)

    def finish(values, lse):
        for i, ref in ((0, a0), (1, a1)):
            ref[...] = values[i].astype(BF)
        lse_out_ref[...] = lse
        for i in (0, 1):
            high_ref[i] = values[i].astype(BF)
        lse_high_ref[...] = lse

    @pl.when(f[2] == 1)
    def _():
        finish((o0[...], o1[...]), lse_ref[...])

    @pl.when(f[2] == 0)
    def _():
        low = half == 0
        lse_c = jnp.where(low, lsec_ref[...], lseb_ref[...])
        lse_l = lse_ref[...]
        top = jnp.maximum(lse_l, lse_c)
        lse = top + jnp.log2(jnp.exp2(lse_l - top) + jnp.exp2(lse_c - top))
        share_l, share_c = jnp.exp2(lse_l - lse), jnp.exp2(lse_c - lse)
        values = []
        for i, ref in ((0, o0), (1, o1)):
            other = jnp.where(low, oc_ref[i], ob_ref[i]).astype(F32)
            rows = []
            for h in range(HALF_HEADS):
                at = slice(h * HEAD_DIM, (h + 1) * HEAD_DIM)
                rows.append(
                    ref[at, :] * share_l[h, i : i + 1] + other[at] * share_c[h, i : i + 1]
                )
            values.append(jnp.concatenate(rows, 0))
        finish(values, lse)


def gradient_tile(
    q_refs, k_refs, v_refs, g_refs, o_refs, lse_ref, dq_refs, dk_acc, dv_acc, unit, at, first
):
    qp, keys = unit
    qs, ks = spans(at, first)
    q, g = q_refs[qp][:, qs], g_refs[qp][:, qs]
    lse = lse_ref[0, qp : qp + 1, qs]
    delta = jnp.sum(g.astype(F32) * o_refs[qp][:, qs].astype(F32), axis=0, keepdims=True)
    dq = None
    for kp in keys:
        k, v = k_refs[kp][:, ks], v_refs[kp][:, ks]
        weights = jnp.exp2(mask_tail(dot(k, q, 0, 0) * SCALE2) - lse)
        ds = (weights * (dot(v, g, 0, 0) - delta)).astype(BF)
        term = dot(k, ds, 1, 0)
        dq = term if dq is None else dq + term
        dk_acc[kp, :, ks] += dot(q, ds, 1, 1)
        dv_acc[kp, :, ks] += dot(g, weights.astype(BF), 1, 1)
    dq_refs[qp][:, qs] = (dq * SCALE).astype(BF)


def local_back_kernel(
    f, q0, q1, k0, k1, v0, v1, g0, g1, o0, o1, lse_ref, d0, d1, dk_acc, dv_acc
):
    dk_acc[...] = jnp.zeros_like(dk_acc)
    dv_acc[...] = jnp.zeros_like(dv_acc)
    sweep(
        f,
        q0.shape[1],
        functools.partial(
            gradient_tile,
            (q0, q1),
            (k0, k1),
            (v0, v1),
            (g0, g1),
            (o0, o1),
            lse_ref,
            (d0.at[0], d1.at[0]),
            dk_acc,
            dv_acc,
        ),
        [unit(f) for unit in LOCAL_UNITS],
    )
    for i, ref in ((0, d0), (1, d1)):
        ref[1] = (dk_acc[i] * SCALE).astype(BF)
        ref[2] = dv_acc[i].astype(BF)


def cross_back_kernel(f, *refs):
    ins, more = refs[:12], refs[12:]
    (ga0, ga1, oa, lse_a, gb0, gb1, ob0, ob1, lse_b, dq_ref, dkv_ref, dk_acc, dv_acc) = more
    dk_acc[...] = jnp.zeros_like(dk_acc)
    dv_acc[...] = jnp.zeros_like(dv_acc)
    for early, at, grads, outs, lse_ref in (
        (1, 0, (ga0, ga1), (oa.at[0], oa.at[1]), lse_a),
        (0, 6, (gb0, gb1), (ob0, ob1), lse_b),
    ):
        q0, q1, k0, k1, v0, v1 = ins[at : at + 6]
        sweep(
            f,
            q0.shape[1],
            functools.partial(
                gradient_tile,
                (q0, q1),
                (k0, k1),
                (v0, v1),
                grads,
                outs,
                lse_ref,
                (dq_ref.at[0], dq_ref.at[1]),
                dk_acc,
                dv_acc,
            ),
            [(f[2] == early, CROSS_UNITS)],
        )
    for i in (0, 1):
        dkv_ref[0, i] = (dk_acc[i] * SCALE).astype(BF)
        dkv_ref[1, i] = dv_acc[i].astype(BF)


def gelu_pair(u):
    k = math.sqrt(2 / math.pi)
    square = u * u
    t = jnp.tanh(k * u * (1.0 + 0.044715 * square))
    half = 0.5 + 0.5 * t
    slope = half + 0.5 * u * (1.0 - t * t) * (k * (1.0 + 3 * 0.044715 * square))
    return u * half, slope


def ff_tile(normed2_ref, cot_ref, wu_ref, wd_ref):
    act, slope = gelu_pair(dot(normed2_ref[...], wu_ref[...], 1, 0))
    act = act.astype(BF)
    grad_up = (dot(cot_ref[...], wd_ref[...], 1, 1) * slope).astype(BF)
    return act, grad_up, dot(act, wd_ref[...], 1, 0), dot(grad_up, wu_ref[...], 1, 1)


def feed_first_kernel(
    f, x_ref, emb_ref, a_ref, b_ref, wa_ref, wb_ref, gain_ref, cot_ref, wu_ref, wd_ref,
    res_ref, n_ref, y_ref, c_ref, dd_ref, du_ref,
):
    step = pl.program_id(0)

    @pl.when(step == 0)
    def _():
        residual = (
            hidden_of(x_ref, emb_ref)
            + dot(a_ref[...], wa_ref[...], 0, 0)
            + dot(b_ref[...], wb_ref[...], 0, 0)
        )
        res_ref[...] = residual
        center, inv = centered(residual)
        n_ref[...] = (center * inv * gain_ref[...]).astype(BF)
        y_ref[...] = residual
        c_ref[...] = jnp.zeros_like(c_ref)

    act, grad_up, y, c = ff_tile(n_ref, cot_ref, wu_ref, wd_ref)
    y_ref[...] += y
    c_ref[...] += c
    dd_ref[...] = dot(act, cot_ref[...], 0, 0).astype(BF)
    du_ref[...] = dot(n_ref[...], grad_up, 0, 0).astype(BF)


def feed_second_kernel(
    f, res_ref, n_ref, y_ref, c_ref, gain_ref, cot_ref, wu_ref, wd_ref, wa_ref, wb_ref, b_ref,
    act_ref, gup_ref, out_ref, gres_ref, gattn_ref, ga_ref, gb_ref, gah_ref, gbh_ref, dgain_ref, dwo_ref,
    y_acc, c_acc,
):
    step = pl.program_id(0)

    @pl.when(step == 0)
    def _():
        y_acc[...] = y_ref[...]
        c_acc[...] = c_ref[...]

    act, grad_up, y, c = ff_tile(n_ref, cot_ref, wu_ref, wd_ref)
    act_ref[...] = act
    gup_ref[...] = grad_up
    y_acc[...] += y
    c_acc[...] += c

    @pl.when(step == pl.num_programs(0) - 1)
    def _():
        out_ref[...] = y_acc[...].astype(BF)
        center, inv = centered(res_ref[...])
        n2 = center * inv
        c_all = c_acc[...]
        dgain_ref[...] = jnp.sum(c_all * n2, axis=0, keepdims=True)
        e = c_all * gain_ref[...]
        grad_residual = cot_ref[...].astype(F32) + inv * (
            e - jnp.mean(e, axis=-1, keepdims=True) - n2 * jnp.mean(e * n2, axis=-1, keepdims=True)
        )
        gres_ref[...] = grad_residual
        grad_attn = grad_residual.astype(BF)
        gattn_ref[...] = grad_attn
        mine = dot(wa_ref[...], grad_attn, 1, 1).astype(BF)
        theirs = dot(wb_ref[...], grad_attn, 1, 1).astype(BF)
        ga_ref[...] = mine
        gb_ref[...] = theirs
        gah_ref[...] = mine[HALF:]
        gbh_ref[...] = theirs[HALF:]
        dwo_ref[...] = dot(b_ref[...], grad_attn, 1, 0).astype(BF)


def combine_kernel(
    f, d0, d1, dqc_ref, dqb_ref, dkvc_ref, dkvb_ref, n0_ref, n1_ref, g0, g1, dw_ref
):
    part = pl.program_id(0)
    late, early = f[2] == 0, f[2] == 1

    def put(low, high):
        for i, (d, g) in enumerate(((d0, g0), (d1, g1))):
            if low is None:
                g[...] = d[0]
            else:
                g[:HALF] = (d[0, :HALF].astype(F32) + low[0, i].astype(F32)).astype(BF)
                g[HALF:] = (d[0, HALF:].astype(F32) + high[0, i].astype(F32)).astype(BF)

    @pl.when(late & (part == 0))
    def _():
        put(dqc_ref, dqb_ref)

    @pl.when(early & (part > 0))
    def _():
        put(dkvb_ref, dkvc_ref)

    @pl.when((late & (part > 0)) | (early & (part == 0)))
    def _():
        put(None, None)

    dw_ref[0] = dot(n0_ref[...], g0[...], 1, 1) + dot(n1_ref[...], g1[...], 1, 1)


def input_grad_kernel(
    f, g_ref, h_ref, wg_ref, wh_ref, x_ref, emb_ref, gain_ref, gres_ref, gin_ref, sums_ref, acc
):
    part = pl.program_id(0)
    value = dot(wg_ref[...], g_ref[...], 1, 0) + dot(wh_ref[...], h_ref[...], 1, 0)

    @pl.when(part == 0)
    def _():
        acc[...] = value

    @pl.when(part > 0)
    def _():
        acc[...] += value

    @pl.when(part == pl.num_programs(0) - 1)
    def _():
        center, inv = centered(hidden_of(x_ref, emb_ref))
        n1 = center * inv
        grad = acc[...].T
        e = grad * gain_ref[...]
        total = gres_ref[...] + inv * (
            e - jnp.mean(e, axis=-1, keepdims=True) - n1 * jnp.mean(e * n1, axis=-1, keepdims=True)
        )
        gin_ref[...] = total.astype(BF)
        sums_ref[...] = jnp.concatenate(
            [jnp.sum(total, axis=0, keepdims=True), jnp.sum(grad * n1, axis=0, keepdims=True)], 0
        )


def swap(array, step):
    axis, mask, size = step
    return lax.ppermute(array, axis, [(i, i ^ mask) for i in range(size)])


def side(step):
    axis, mask, _ = step
    return (lax.axis_index(axis) // mask) % 2


def halve(total, step):
    here, half = side(step), total.shape[0] // 2
    sent = lax.dynamic_slice_in_dim(total, (1 - here) * half, half, 0).astype(BF)
    kept = lax.dynamic_slice_in_dim(total, here * half, half, 0)
    return kept.astype(F32) + swap(sent, step).astype(F32)


def join(own, other, step, axis=0):
    return jnp.where(
        side(step) == 0,
        jnp.concatenate([own, other], axis),
        jnp.concatenate([other, own], axis),
    )


def sum_over(total, steps):
    for step in steps:
        total = halve(total, step)
    total = total.astype(BF)
    for step in reversed(steps):
        total = join(total, swap(total, step), step)
    return total


def on_device(
    sizes, block_input, segments, pass_emb, gain_attn, w_qkv, w_out, gain_mlp, w_up, w_down, cotangent
):
    passes, n_dp = sizes
    core = ("pass", 1, passes)
    cross = ("pass", 2, passes)
    lanes = [("dp", 1 << i, n_dp) for i in range(n_dp.bit_length() - 1)]
    order_a = lanes[:1] + [cross] + lanes[1:]
    order_b = lanes[1:] + lanes[:1] + [cross]
    order_c = [cross] + lanes

    pass_here = lax.axis_index("pass")
    core_here = pass_here % 2
    length = segments.shape[0]
    flags = jnp.stack(
        [
            (segments[0] == segments[length - 1]).astype(jnp.int32),
            core_here.astype(jnp.int32),
            (pass_here < 2).astype(jnp.int32),
            pass_here.astype(jnp.int32),
        ]
    )

    def to_late(array, other=0):
        return lax.ppermute(array, "pass", [(0, 2 + other), (1, 3 - other)])

    def to_early(array, other=0):
        return lax.ppermute(array, "pass", [(2, other), (3, 1 - other)])

    x, cot = block_input[0], cotangent[0]
    emb = (pass_emb.reshape(passes, 1, D), (1, 1, D), lambda i, f: (f[3], 0, 0))

    normed, theirs, low_t, high_t = call(
        norm_project_kernel,
        flags,
        (3,),
        [
            fixed(x),
            emb,
            fixed(row(gain_attn)),
            (w_qkv, (D, GROUP), lambda i, f: (0, 2 * i + 1 - f[1])),
        ],
        [out_fixed((D, length), BF)] + projection_outs(length),
        5,
        "norm_project",
    )
    other = swap(theirs, core)
    own, low_o, high_o = call(
        project_kernel,
        flags,
        (3,),
        [fixed(normed), (w_qkv, (D, GROUP), lambda i, f: (0, 2 * i + f[1]))],
        projection_outs(length),
        3,
        "project_own",
    )
    late_kv = (to_late(low_o), to_late(low_t, 1))
    early_q = (to_early(high_o), to_early(high_t, 1))
    normed_other = swap(normed, core)

    local_inputs = [head(a, at) for at in (0, 6, 12) for a in (own, other)]
    o0, o1, lse_local = call(
        local_kernel,
        flags,
        (HEADS // 2,),
        local_inputs,
        [((GROUP, length), F32, (HEAD_DIM, length), lambda h, f: (h, 0))] * 2
        + [lse_out(HEADS // 2, length)],
        14,
        "attend_local",
    )
    cross_in = cross_inputs(early_q, own, other, late_kv)
    pair_out = ((2, HALF, length), BF, (2, HEAD_DIM, length), lambda h, f: (0, h, 0))
    o_cross, lse_cross = call(
        cross_kernel,
        flags,
        (HALF_HEADS,),
        cross_in,
        [pair_out, lse_out(HALF_HEADS, length)],
        11,
        "attend_cross",
    )
    o_back, lse_back = to_late(o_cross), to_late(lse_cross)
    half_rows = (HALF, length)
    att_own, att_pair, lse, att_high, lse_high = call(
        merge_kernel,
        flags,
        (2,),
        [
            (o0, half_rows, lambda i, f: (i, 0)),
            (o1, half_rows, lambda i, f: (i, 0)),
            (lse_local, (HALF_HEADS, 2, length), lambda i, f: (i, 0, 0)),
            fixed(o_cross),
            fixed(lse_cross),
            fixed(o_back),
            fixed(lse_back),
        ],
        [((GROUP, length), BF, half_rows, lambda i, f: (i, 0))] * 2
        + [
            ((HEADS // 2, 2, length), F32, (HALF_HEADS, 2, length), lambda i, f: (i, 0, 0)),
            out_fixed((2, HALF, length), BF),
            out_fixed((HALF_HEADS, 2, length), F32),
        ],
        3,
        "merge",
    )
    att_other = swap(att_pair, core)
    att_early, lse_early = to_early(att_high), to_early(lse_high)

    w_half = [(w_out, (GROUP, D), lambda i, f: (f[1], 0)), (w_out, (GROUP, D), lambda i, f: (1 - f[1], 0))]
    ff_half = w_up.shape[1] // 2
    steps = ff_half // FF_TILE

    def ff_weights(at):
        return [
            (w_up, (D, FF_TILE), lambda i, f: (0, at(f) * steps + i)),
            (w_down, (FF_TILE, D), lambda i, f: (at(f) * steps + i, 0)),
        ]

    tokens = (length, D)
    residual, normed2, y_part, c_part, down_sent, up_sent = call(
        feed_first_kernel,
        flags,
        (steps,),
        [fixed(x), emb, fixed(att_own), fixed(att_other)]
        + w_half
        + [fixed(row(gain_mlp)), fixed(cot)]
        + ff_weights(lambda f: 1 - f[1]),
        [
            out_fixed(tokens, F32),
            out_fixed(tokens, BF),
            out_fixed(tokens, F32),
            out_fixed(tokens, F32),
            ((ff_half, D), BF, (FF_TILE, D), lambda i, f: (i, 0)),
            ((D, ff_half), BF, (D, FF_TILE), lambda i, f: (0, i)),
        ],
        16,
        "feed_first",
        56,
    )
    down_recv, up_recv = swap(down_sent, core), swap(up_sent, core)
    (
        act, grad_up, output, grad_residual, grad_attn, g_own, g_theirs, g_own_high, g_theirs_high, dgain_mlp, out_sent
    ) = call(
        feed_second_kernel,
        flags,
        (steps,),
        [fixed(a) for a in (residual, normed2, y_part, c_part, row(gain_mlp), cot)]
        + ff_weights(lambda f: f[1])
        + w_half
        + [fixed(att_other)],
        [
            ((length, ff_half), BF, (length, FF_TILE), lambda i, f: (0, i)),
            ((length, ff_half), BF, (length, FF_TILE), lambda i, f: (0, i)),
            out_fixed(tokens, BF),
            out_fixed(tokens, F32),
            out_fixed(tokens, BF),
            out_fixed((GROUP, length), BF),
            out_fixed((GROUP, length), BF),
            out_fixed(half_rows, BF),
            out_fixed(half_rows, BF),
            out_fixed((1, D), F32),
            out_fixed((GROUP, D), BF),
        ],
        16,
        "feed_second",
        56,
        [pltpu.VMEM(tokens, F32)] * 2,
    )
    g_other = swap(g_theirs, core)
    early_g = (to_early(g_own_high), to_early(g_theirs_high, 1))
    down_half = dot(act, cot, 0, 0) + down_recv.astype(F32)
    up_half = dot(normed2, grad_up, 0, 0) + up_recv.astype(F32)
    out_half = dot(att_own, grad_attn, 1, 0) + swap(out_sent, core).astype(F32)

    accumulators = [pltpu.VMEM((2, HEAD_DIM, length), F32)] * 2
    dq_cross, dkv_cross = call(
        cross_back_kernel,
        flags,
        (HALF_HEADS,),
        cross_in
        + [
            head(early_g[0], 0),
            head(early_g[1], 0),
            (att_early, (2, HEAD_DIM, length), lambda h, f: (0, h, 0)),
            lse_spec(lse_early),
            head(g_own, 0),
            head(g_other, 0),
            head(att_own, 0),
            head(att_pair, 0),
            lse_spec(lse),
        ],
        [
            pair_out,
            (
                (2, 2, HALF, length),
                BF,
                (2, 2, HEAD_DIM, length),
                lambda h, f: (0, 0, h, 0),
            ),
        ],
        16,
        "attend_back_cross",
        48,
        accumulators,
    )
    dq_back, dkv_back = to_late(dq_cross), to_early(dkv_cross)
    d_own, d_pair = call(
        local_back_kernel,
        flags,
        (HEADS // 2,),
        local_inputs
        + [head(a, 0) for a in (g_own, g_other, att_own, att_pair)]
        + [lse_spec(lse)],
        [((3, GROUP, length), BF, (3, HEAD_DIM, length), lambda h, f: (0, h, 0))] * 2,
        25,
        "attend_back_local",
        48,
        accumulators,
    )
    part_block = (1, GROUP, length)
    one_q = (1, 2, HALF, length)
    gp_own, gp_pair, dw_parts = call(
        combine_kernel,
        flags,
        (3,),
        [
            (d_own, part_block, lambda i, f: (i, 0, 0)),
            (d_pair, part_block, lambda i, f: (i, 0, 0)),
            fixed(dq_cross.reshape(one_q)),
            fixed(dq_back.reshape(one_q)),
            (dkv_cross, one_q, lambda i, f: (jnp.maximum(i - 1, 0), 0, 0, 0)),
            (dkv_back, one_q, lambda i, f: (jnp.maximum(i - 1, 0), 0, 0, 0)),
            fixed(normed),
            fixed(normed_other),
        ],
        [((3 * GROUP, length), BF, (GROUP, length), lambda i, f: (i, 0))] * 2
        + [((3, D, GROUP), F32, (1, D, GROUP), lambda i, f: (i, 0, 0))],
        6,
        "combine",
    )
    gp_other = swap(gp_pair, core)
    grad_input, sums = call(
        input_grad_kernel,
        flags,
        (3,),
        [
            (gp_own, (GROUP, length), lambda i, f: (i, 0)),
            (gp_other, (GROUP, length), lambda i, f: (i, 0)),
            (w_qkv, (D, GROUP), lambda i, f: (0, 2 * i + f[1])),
            (w_qkv, (D, GROUP), lambda i, f: (0, 2 * i + 1 - f[1])),
            fixed(x),
            emb,
            fixed(row(gain_attn)),
            fixed(grad_residual),
        ],
        [out_fixed(tokens, BF), out_fixed((2, D), F32)],
        6,
        "input_grad",
        48,
        [pltpu.VMEM((D, length), F32)],
    )
    selector = (jnp.arange(passes) == pass_here).astype(F32)
    small = jnp.concatenate([selector[:, None] * sums[:1], sums[1:], dgain_mlp])
    for step in [core, cross] + lanes:
        small = small + swap(small, step)

    def whole(half, steps, axis=0):
        half = sum_over(half, steps)
        return join(half, swap(half, core), core, axis).astype(F32)

    down_total = whole(down_half, order_a)
    up_total = whole(up_half, order_b, 1)
    out_total = whole(out_half, order_c)
    qkv_total = jnp.concatenate(
        [whole(dw_parts[i], order, 1) for i, order in enumerate((order_a, order_b, order_c))],
        axis=1,
    )
    return (
        output[None],
        grad_input[None],
        small[:passes],
        small[passes],
        qkv_total,
        out_total,
        small[passes + 1],
        up_total,
        down_total,
    )


def solution(mesh):
    sizes = (mesh.shape["pass"], mesh.shape["dp"])
    tokens = P("pass", "dp", None)
    in_specs = (tokens, P("dp")) + (P(),) * 7 + (tokens,)
    out_specs = (tokens, tokens) + (P(),) * 7
    return jax.shard_map(
        functools.partial(on_device, sizes),
        mesh=mesh,
        in_specs=in_specs,
        out_specs=out_specs,
        check_vma=False,
    )
```

time: 567 us -> 501 us (0.88)
  Pallas kernels: 45.7 us -> 118 us
  matrix products: 72.9 us -> 7.9 us
  local copies, waits for them, and re-layouts: 70.6 us -> 21.5 us
  other arithmetic: 50 us -> 21 us
  starting transfers between devices: 95.1 us -> 112 us
  waiting for transfers between devices: 220 us -> 208 us
    pallas_call x4 -> x11, Pallas kernels: 45.7 us -> 118 us  [call(): pl.pallas_call(kernel, grid_spec=pltpu.PrefetchScalarGridSpec(num_scalar_...]
    dot_general x22 -> x3, matrix products: 72.9 us -> 7.9 us  [dot(): lax.dot_general(a, b, (((ca,), (cb,)), ((), ())), preferred_element_type=...]
    unnamed x126 -> x84, local copies, waits for them, and re-layouts: 39.4 us -> 13.8 us
    ppermute x66 -> x67, waiting for transfers between devices: 192 us -> 173 us  [swap(): return lax.ppermute(array, axis, [(i, i ^ mask) for i in range(size)])]
    dynamic_slice x3 -> x0, local copies, waits for them, and re-layouts: 18.1 us -> none  [the longest x1 13.3 us: on_device(): own = lax.dynamic_index_in_dim(projected, core_here, 1, keepdims=False)]
    ppermute x66 -> x67, starting transfers between devices: 76.9 us -> 89.3 us  [swap(): return lax.ppermute(array, axis, [(i, i ^ mask) for i in range(size)])]
    ppermute x8 -> x12, waiting for transfers between devices: 28 us -> 34.8 us  [the longest x7 29.4 us: to_early(): return lax.ppermute(array, 'pass', [(2, other), (3, 1 - other)])]
    convert_element_type x3, other arithmetic: 16.5 us -> 10.3 us  [whole(): return join(half, swap(half, core), core, axis).astype(F32)]
  transfers between devices with their start and end apart: 74 -> 79, of which waited for: 38 -> 35; matrix products, arithmetic and copies ran while one was open for 25% -> 5% of each run, Pallas kernels for 8% -> 13%
where the time goes in v2:
time: 501 us; the launch traced here: 492 us
  waiting for transfers between devices  208 us (42%)
  Pallas kernels  118 us (24%)
  starting transfers between devices  112 us (22%)
  local copies, waits for them, and re-layouts  21.5 us (4%)
  other arithmetic  21 us (4%)
  matrix products  7.9 us (2%)
    ppermute x67, waiting for transfers between devices, swap(): return lax.ppermute(array, axis, [(i, i ^ mask) for i in range(size)])  173 us
    pallas_call x11, Pallas kernels, call(): pl.pallas_call(kernel, grid_spec=pltpu.PrefetchScalarGridSpec(num_scalar_...  118 us
    ppermute x67, starting transfers between devices, swap(): return lax.ppermute(array, axis, [(i, i ^ mask) for i in range(size)])  89.3 us
    ppermute x7, waiting for transfers between devices, to_early(): return lax.ppermute(array, 'pass', [(2, other), (3, 1 - other)])  29.4 us
    unnamed x84, local copies, waits for them, and re-layouts  13.8 us
    ppermute x5, starting transfers between devices, to_late(): return lax.ppermute(array, 'pass', [(0, 2 + other), (1, 3 - other)])  13.3 us
    convert_element_type x3, other arithmetic, whole(): return join(half, swap(half, core), core, axis).astype(F32)  10.3 us
  transfers between devices with their start and end apart: 79, of which 35 were waited for; matrix products, arithmetic and copies ran while one was open for 5% of the time, Pallas kernels for 13%

profile of v2, /device:TPU:0, one launch (start us, length us, event | category | flops | bytes accessed | tf_op | source)
XLA Modules:
  0.0 491.9 jit_solution(2764532457950134177)
XLA Ops:
  6.1 5.1 %norm_project.1 = (bf16[768,768]{1,0:T(8,128)(2,1)S(1)}, bf16[1152,768]{1,0:T(8,128)(2,1)S(1)}, bf16[384,768]{1,0:T(8,128)(2,1)S(1)}, bf16[192,768]{1,0:T(8,128)(2,1)S(1)}) custom-call(s32[4]{0:T(128)S(1)} %pad_add_fusion.f, bf16[768,768]{1,0:T(8,128)(2,1)S(1)} %bitcast.29, f32[4,1,768]{2,1,0:T(1,128)S(1)} %reshape.52.emb_ref, ...), custom_call_target="tpu_custom_call" | custom-call | flops 5500000256 | bytes 1048576 | tf_op jit(solution)/shard_map/norm_project/pallas_call | solution.py:39
  11.7 4.5 collective-permute-start.4
  16.3 4.1 project_own.1
  24.3 8.3 %collective-permute-done.2.refs_1_ = bf16[192,768]{1,0:T(8,128)(2,1)S(1)} collective-permute-done((bf16[192,768]{1,0:T(8,128)(2,1)S(1)}, bf16[192,768]{1,0:T(8,128)(2,1)S(1)}, u32[]{:S(2)}, u32[]{:S(2)}) %collective-permute-start.2) | collective-permute-done | bytes 294944 | tf_op jit(solution)/shard_map/ppermute | solution.py:530
  32.6 6.6 %collective-permute-done.1.refs_0_ = bf16[192,768]{1,0:T(8,128)(2,1)S(1)} collective-permute-done((bf16[192,768]{1,0:T(8,128)(2,1)S(1)}, bf16[192,768]{1,0:T(8,128)(2,1)S(1)}, u32[]{:S(2)}, u32[]{:S(2)}) %collective-permute-start.1) | collective-permute-done | bytes 294944 | tf_op jit(solution)/shard_map/ppermute | solution.py:530
  39.2 2.7 collective-permute-done.3.refs_8_.refs_10_
  41.9 7.0 %attend_cross.1 = (bf16[2,192,768]{2,1,0:T(8,128)(2,1)S(1)}, f32[3,2,768]{2,1,0:T(2,128)S(1)}) custom-call(s32[4]{0:T(128)S(1)} %pad_add_fusion.f, bf16[192,768]{1,0:T(8,128)(2,1)S(1)} %collective-permute-done.1.refs_0_, bf16[192,768]{1,0:T(8,128)(2,1)S(1)} %collective-permute-done.2.refs_1_, ...), custom_call_target="tpu_custom_call" | custom-call | flops 12099999744 | bytes 1048576 | tf_op jit(solution)/shard_map/attend_cross/pallas_call | solution.py:39
  48.9 4.4 collective-permute-start.6
  54.9 9.3 %attend_local.1 = (f32[384,768]{1,0:T(8,128)S(1)}, f32[384,768]{1,0:T(8,128)S(1)}, f32[6,2,768]{2,1,0:T(2,128)S(1)}) custom-call(s32[4]{0:T(128)S(1)} %pad_add_fusion.f, bf16[1152,768]{1,0:T(8,128)(2,1)S(1)} %get-tuple-element.53.q0.k0.v0.refs_2_.refs_4_.refs_6_, bf16[1152,768]{1,0:T(8,128)(2,1)S(1)} %collective-permute-done.q1.k1.v1.refs_3_.refs_5_.refs_7_, ...), custom_call_target="tpu_custom_call" | custom-call | flops 15399999488 | bytes 1048576 | tf_op jit(solution)/shard_map/attend_local/pallas_call | solution.py:39
  64.3 2.8 collective-permute-done.5.ob_ref
  72.9 18.7 %feed_first.1 = (f32[768,768]{1,0:T(8,128)}, bf16[768,768]{1,0:T(8,128)(2,1)}, f32[768,768]{1,0:T(8,128)}, f32[768,768]{1,0:T(8,128)}, bf16[1536,768]{1,0:T(8,128)(2,1)}, /*index=5*/bf16[768,1536]{1,0:T(8,128)(2,1)}) custom-call(s32[4]{0:T(128)} %copy-done.6, bf16[768,768]{1,0:T(8,128)(2,1)} %bitcast.28, f32[4,1,768]{2,1,0:T(1,128)} %copy-done.2, ...), custom_call_target="tpu_custom_call" | custom-call | flops 17600000000 | bytes 1048576 | tf_op jit(solution)/shard_map/feed_first/pallas_call | solution.py:39
  91.7 21.7 %feed_second.1 = (bf16[768,1536]{1,0:T(8,128)(2,1)}, bf16[768,1536]{1,0:T(8,128)(2,1)}, bf16[768,768]{1,0:T(8,128)(2,1)}, f32[768,768]{1,0:T(8,128)}, bf16[768,7...) custom-call(s32[4]{0:T(128)} %copy-done.6, ...), custom_call_target="tpu_custom_call" | custom-call | flops 17600000000 | bytes 1048576 | tf_op jit(solution)/shard_map/feed_second/pallas_call | solution.py:39
  113.5 2.2 collective-permute-done.49
  115.7 1.9 convolution_add_fusion
  118.7 2.9 collective-permute-start.50
  121.6 7.3 %collective-permute-done.50 = bf16[192,768]{1,0:T(8,128)(2,1)S(1)} collective-permute-done((bf16[192,768]{1,0:T(8,128)(2,1)S(1)}, bf16[192,768]{1,0:T(8,128)(2,1)S(1)}, u32[]{:S(2)}, u32[]{:S(2)}) %collective-permute-start.50) | collective-permute-done | bytes 294944 | tf_op jit(solution)/shard_map/ppermute | solution.py:471
  130.1 6.1 %collective-permute-start.51 = (bf16[96,768]{1,0:T(8,128)(2,1)S(1)}, bf16[96,768]{1,0:T(8,128)(2,1)S(1)}, u32[]{:S(2)}, u32[]{:S(2)}) collective-permute-start(bf16[96,768]{1,0:T(8,128)(2,1)S(1)} %dynamic-slice_convert_fusion.12), channel_id=1, source_target_pairs={{0,1},{1,0},{2,3},{3,2},{4,5},{5,4},{6,7},{7,6},{8,9},{9,8},{10,11... | collective-permute-start | bytes 442376 | tf_op jit(solution)/shard_map/ppermute | solution.py:471
  136.1 3.3 collective-permute-done.51
  144.0 2.7 collective-permute-start.53
  149.3 2.3 collective-permute-start.54
  151.6 2.6 collective-permute-done.54
  155.5 14.4 %collective-permute-done.12.refs_15_ = f32[3,2,768]{2,1,0:T(2,128)S(1)} collective-permute-done((f32[3,2,768]{2,1,0:T(2,128)S(1)}, f32[3,2,768]{2,1,0:T(2,128)S(1)}, u32[]{:S(2)}, u32[]{:S(2)}) %collective-permute-start.12) | collective-permute-done | bytes 18464 | tf_op jit(solution)/shard_map/ppermute | solution.py:530
  176.8 13.6 %attend_back_cross.1 = (bf16[2,192,768]{2,1,0:T(8,128)(2,1)S(1)}, bf16[2,2,192,768]{3,2,1,0:T(8,128)(2,1)}) custom-call(s32[4]{0:T(128)S(1)} %copy-done.7, bf16[192,768]{1,0:T(8,128)(2,1)S(1)} %copy-done.22, bf16[192,768]{1,0:T(8,128)(2,1)S(1)} %copy-done.20, bf16[1152,768]{1,0:T(8,128)(2,1)} %copy-done.23, bf16[1152,768]{1,0:T(8,128)(2,1)} %copy-done.8, ...), custom_call_target="tpu_custom_call" | custom-call | flops 17600000000 | bytes 1048576 | tf_op jit(solution)/shard_map/attend_back_cross/pallas_call | solution.py:39
  193.3 6.8 %collective-permute-start.56 = (bf16[96,768]{1,0:T(8,128)(2,1)S(1)}, bf16[96,768]{1,0:T(8,128)(2,1)S(1)}, u32[]{:S(2)}, u32[]{:S(2)}) collective-permute-start(bf16[96,768]{1,0:T(8,128)(2,1)S(1)} %maximum_select_fusion.25), channel_id=1, source_target_pairs={{0,1},{1,0},{2,3},{3,2},{4,5},{5,4},{6,7},{7,6},{8,9},{9,8},{10,11... | collective-permute-start | bytes 442376 | tf_op jit(solution)/shard_map/ppermute | solution.py:471
  200.0 18.4 %attend_back_local.1 = (bf16[3,384,768]{2,1,0:T(8,128)(2,1)S(1)}, bf16[3,384,768]{2,1,0:T(8,128)(2,1)S(1)}) custom-call(s32[4]{0:T(128)S(1)} %copy-done.7, bf16[1152,768]{1,0:T(8,128)(2,1)} %copy-done.23, bf16[1152,768]{1,0:T(8,128)(2,1)} %copy-done.8, bf16[1152,768]{1,0:T(8,128)(2,1)} %copy-done.23, bf16[1152,768]{1,0:T(8,128)(2,1)} %copy-done.8, ...), custom_call_target="tpu_custom_call" | custom-call | flops 27499999232 | bytes 1048576 | tf_op jit(solution)/shard_map/attend_back_local/pallas_call | solution.py:39
  221.0 2.8 collective-permute-start.57
  223.7 8.1 %combine.1 = (bf16[1152,768]{1,0:T(8,128)(2,1)}, bf16[1152,768]{1,0:T(8,128)(2,1)}, f32[3,768,384]{2,1,0:T(8,128)}) custom-call(s32[4]{0:T(128)S(1)} %copy-done.7, bf16[3,384,768]{2,1,0:T(8,128)(2,1)} %copy-done.25, bf16[3,384,768]{2,1,0:T(8,128)(2,1)} %copy-done.26, bf16[1,2,192,768]{3,2,1,0:T(8,128)(2,1)S(1)} %bitcast.31, ...), custom_call_target="tpu_custom_call" | custom-call | flops 6600000000 | bytes 1048576 | tf_op jit(solution)/shard_map/combine/pallas_call | solution.py:39
  231.8 2.2 fusion.8
  236.7 6.6 %collective-permute-done.31 = bf16[384,384]{1,0:T(8,128)(2,1)S(1)} collective-permute-done((bf16[384,384]{1,0:T(8,128)(2,1)S(1)}, bf16[384,384]{1,0:T(8,128)(2,1)S(1)}, u32[]{:S(2)}, u32[]{:S(2)}) %collective-permute-start.31) | collective-permute-done | bytes 294944 | tf_op jit(solution)/shard_map/ppermute | solution.py:471
  243.3 8.8 %collective-permute-start.22 = (bf16[384,384]{1,0:T(8,128)(2,1)S(1)}, bf16[384,384]{1,0:T(8,128)(2,1)S(1)}, u32[]{:S(2)}, u32[]{:S(2)}) collective-permute-start(bf16[384,384]{1,0:T(8,128)(2,1)S(1)} %fusion.3), channel_id=1, source_target_pairs={{0,1},{1,0},{2,3},{3,2},{4,5},{5,4},{6,7},{7,6},{8,9},{9,8},{10,11... | collective-permute-start | bytes 884744 | tf_op jit(solution)/shard_map/ppermute | solution.py:471
  252.2 4.5 collective-permute-start.32
  260.0 3.7 collective-permute-done.32
  265.0 3.8 collective-permute-done.23
  271.1 2.1 collective-permute-done.42
  273.6 2.4 collective-permute-start.43
  276.0 3.9 convert_add_fusion.1
  283.7 3.0 collective-permute-start.44
  286.6 2.1 convert_add_fusion
  288.7 17.7 %collective-permute-done.60 = bf16[384,1536]{1,0:T(8,128)(2,1)S(1)} collective-permute-done((bf16[384,1536]{1,0:T(8,128)(2,1)S(1)}, bf16[384,1536]{1,0:T(8,128)(2,1)S(1)}, u32[]{:S(2)}, u32[]{:S(2)}) %collective-permute-start.60) | collective-permute-done | bytes 1179680 | tf_op jit(solution)/shard_map/ppermute | solution.py:471
  307.8 3.0 collective-permute-start.26
  312.3 21.3 %collective-permute-done.26 = bf16[48,384]{1,0:T(8,128)(2,1)S(1)} collective-permute-done((bf16[48,384]{1,0:T(8,128)(2,1)S(1)}, bf16[48,384]{1,0:T(8,128)(2,1)S(1)}, u32[]{:S(2)}, u32[]{:S(2)}) %collective-permute-start.26) | collective-permute-done | bytes 36896 | tf_op jit(solution)/shard_map/ppermute | solution.py:471
  337.0 7.3 %collective-permute-done.62 = bf16[96,1536]{1,0:T(8,128)(2,1)S(1)} collective-permute-done((bf16[96,1536]{1,0:T(8,128)(2,1)S(1)}, bf16[96,1536]{1,0:T(8,128)(2,1)S(1)}, u32[]{:S(2)}, u32[]{:S(2)}) %collective-permute-start.62) | collective-permute-done | bytes 294944 | tf_op jit(solution)/shard_map/ppermute | solution.py:471
  344.3 1.9 collective-permute-start.71
  346.2 11.9 %collective-permute-done.71 = bf16[384,768]{1,0:T(8,128)(2,1)S(1)} collective-permute-done((bf16[384,768]{1,0:T(8,128)(2,1)S(1)}, bf16[384,768]{1,0:T(8,128)(2,1)S(1)}, u32[]{:S(2)}, u32[]{:S(2)}) %collective-permute-start.71) | collective-permute-done | bytes 589856 | tf_op jit(solution)/shard_map/ppermute | solution.py:471
  360.1 3.2 collective-permute-done.63
  363.8 6.2 %collective-permute-done.72 = bf16[192,768]{1,0:T(8,128)(2,1)S(1)} collective-permute-done((bf16[192,768]{1,0:T(8,128)(2,1)S(1)}, bf16[192,768]{1,0:T(8,128)(2,1)S(1)}, u32[]{:S(2)}, u32[]{:S(2)}) %collective-permute-start.72) | collective-permute-done | bytes 294944 | tf_op jit(solution)/shard_map/ppermute | solution.py:471
  371.9 3.3 collective-permute-done.64
  375.2 1.9 collective-permute-start.73
  377.7 8.0 %collective-permute-done.73 = bf16[96,768]{1,0:T(8,128)(2,1)S(1)} collective-permute-done((bf16[96,768]{1,0:T(8,128)(2,1)S(1)}, bf16[96,768]{1,0:T(8,128)(2,1)S(1)}, u32[]{:S(2)}, u32[]{:S(2)}) %collective-permute-start.73) | collective-permute-done | bytes 147488 | tf_op jit(solution)/shard_map/ppermute | solution.py:471
  386.7 14.1 %collective-permute-done.74 = bf16[96,768]{1,0:T(8,128)(2,1)S(1)} collective-permute-done((bf16[96,768]{1,0:T(8,128)(2,1)S(1)}, bf16[96,768]{1,0:T(8,128)(2,1)S(1)}, u32[]{:S(2)}, u32[]{:S(2)}) %collective-permute-start.74) | collective-permute-done | bytes 147488 | tf_op jit(solution)/shard_map/ppermute | solution.py:471
  405.7 5.7 %collective-permute-done.75 = bf16[192,768]{1,0:T(8,128)(2,1)S(1)} collective-permute-done((bf16[192,768]{1,0:T(8,128)(2,1)S(1)}, bf16[192,768]{1,0:T(8,128)(2,1)S(1)}, u32[]{:S(2)}, u32[]{:S(2)}) %collective-permute-start.75) | collective-permute-done | bytes 294944 | tf_op jit(solution)/shard_map/ppermute | solution.py:471
  413.1 9.5 %collective-permute-done.66 = bf16[192,1536]{1,0:T(8,128)(2,1)S(1)} collective-permute-done((bf16[192,1536]{1,0:T(8,128)(2,1)S(1)}, bf16[192,1536]{1,0:T(8,128)(2,1)S(1)}, u32[]{:S(2)}, u32[]{:S(2)}) %collective-permute-start.66) | collective-permute-done | bytes 589856 | tf_op jit(solution)/shard_map/ppermute | solution.py:471
  422.6 1.9 collective-permute-start.76
  426.2 7.2 %collective-permute-done.76 = bf16[384,768]{1,0:T(8,128)(2,1)S(1)} collective-permute-done((bf16[384,768]{1,0:T(8,128)(2,1)S(1)}, bf16[384,768]{1,0:T(8,128)(2,1)S(1)}, u32[]{:S(2)}, u32[]{:S(2)}) %collective-permute-start.76) | collective-permute-done | bytes 589856 | tf_op jit(solution)/shard_map/ppermute | solution.py:471
  435.1 10.7 %input_grad.1 = (bf16[768,768]{1,0:T(8,128)(2,1)}, f32[2,768]{1,0:T(2,128)S(1)}) custom-call(s32[4]{0:T(128)S(1)} %copy-done.7, bf16[1152,768]{1,0:T(8,128)(2,1)S(1)} %copy-done.24, bf16[1152,768]{1,0:T(8,128)(2,1)S(1)} %collective-permute-done.16.h_ref, bf16[768,2304]{1,0:T(8,128)(2,1)} %wh_ref.1, bf16[768,2304]{1,0:T(8,128)(2,1)} %wh_ref.1, ...), custom_call_target="tpu_custom_call" | custom-call | flops 6600000000 | bytes 1048576 | tf_op jit(solution)/shard_map/input_grad/pallas_call | solution.py:39
  445.8 6.8 %collective-permute-done.67 = bf16[384,1536]{1,0:T(8,128)(2,1)S(1)} collective-permute-done((bf16[384,1536]{1,0:T(8,128)(2,1)S(1)}, bf16[384,1536]{1,0:T(8,128)(2,1)S(1)}, u32[]{:S(2)}, u32[]{:S(2)}) %collective-permute-start.67) | collective-permute-done | bytes 1179680 | tf_op jit(solution)/shard_map/ppermute | solution.py:471
  453.4 4.1 collective-permute-done.77
  459.3 4.4 collective-permute-done.17
  467.1 2.3 collective-permute-done.18
  470.5 2.8 collective-permute-done.19
  475.1 1.9 collective-permute-done.20
  478.4 3.2 maximum_convert_fusion
  483.0 4.4 fusion
  487.5 4.2 fusion.1
  (288 shorter events, 85.6 us)
Async XLA Ops:
  11.2 30.7 %collective-permute-start = (bf16[1152,768]{1,0:T(8,128)(2,1)S(1)}, bf16[1152,768]{1,0:T(8,128)(2,1)S(1)}, u32[]{:S(2)}, u32[]{:S(2)}) collective-permute-start(bf16[1152,768]{1,0:T(8,128)(2,1)S(1)} %get-tuple-element.54), channel_id=1, source_target_pairs={{0,8},{8,0},{16,24},{24,16},{1,9},{9,1},{17,25},{25,17},{2,10},{10... | collective-permute-start | bytes 5308424 | tf_op jit(solution)/shard_map/ppermute | solution.py:471
  11.7 27.5 %collective-permute-start.4 = (bf16[384,768]{1,0:T(8,128)(2,1)S(1)}, bf16[384,768]{1,0:T(8,128)(2,1)S(1)}, u32[]{:S(2)}, u32[]{:S(2)}) collective-permute-start(bf16[384,768]{1,0:T(8,128)(2,1)S(1)} %get-tuple-element.61), channel_id=1, source_target_pairs={{0,24},{8,16},{1,25},{9,17},{2,26},{10,18},{3,27},{11,19},{4,28},{... | collective-permute-start | bytes 1769480 | tf_op jit(solution)/shard_map/ppermute | solution.py:527
  20.4 21.5 %collective-permute-start.3 = (bf16[384,768]{1,0:T(8,128)(2,1)S(1)}, bf16[384,768]{1,0:T(8,128)(2,1)S(1)}, u32[]{:S(2)}, u32[]{:S(2)}) collective-permute-start(bf16[384,768]{1,0:T(8,128)(2,1)S(1)} %get-tuple-element.60), channel_id=1, source_target_pairs={{0,16},{8,24},{1,17},{9,25},{2,18},{10,26},{3,19},{11,27},{4,20},{... | collective-permute-start | bytes 1769480 | tf_op jit(solution)/shard_map/ppermute | solution.py:527
  21.7 10.9 %collective-permute-start.2 = (bf16[192,768]{1,0:T(8,128)(2,1)S(1)}, bf16[192,768]{1,0:T(8,128)(2,1)S(1)}, u32[]{:S(2)}, u32[]{:S(2)}) collective-permute-start(bf16[192,768]{1,0:T(8,128)(2,1)S(1)} %get-tuple-element.59), channel_id=1, source_target_pairs={{16,8},{24,0},{17,9},{25,1},{18,10},{26,2},{19,11},{27,3},{20,12},... | collective-permute-start | bytes 884744 | tf_op jit(solution)/shard_map/ppermute | solution.py:530
  23.0 16.2 %collective-permute-start.1 = (bf16[192,768]{1,0:T(8,128)(2,1)S(1)}, bf16[192,768]{1,0:T(8,128)(2,1)S(1)}, u32[]{:S(2)}, u32[]{:S(2)}) collective-permute-start(bf16[192,768]{1,0:T(8,128)(2,1)S(1)} %get-tuple-element.58), channel_id=1, source_target_pairs={{16,0},{24,8},{17,1},{25,9},{18,2},{26,10},{19,3},{27,11},{20,4},{... | collective-permute-start | bytes 884744 | tf_op jit(solution)/shard_map/ppermute | solution.py:530
  48.9 15.3 %collective-permute-start.6 = (f32[3,2,768]{2,1,0:T(2,128)S(1)}, f32[3,2,768]{2,1,0:T(2,128)S(1)}, u32[]{:S(2)}, u32[]{:S(2)}) collective-permute-start(f32[3,2,768]{2,1,0:T(2,128)S(1)} %get-tuple-element.63.lsec_ref), channel_id=1, source_target_pairs={{0,16},{8,24},{1,17},{9,25},{2,18},{10,26},{3,19},{11,27},{4,20},{... | collective-permute-start | bytes 55304 | tf_op jit(solution)/shard_map/ppermute | solution.py:527
  53.3 13.7 %collective-permute-start.5 = (bf16[2,192,768]{2,1,0:T(8,128)(2,1)S(1)}, bf16[2,192,768]{2,1,0:T(8,128)(2,1)S(1)}, u32[]{:S(2)}, u32[]{:S(2)}) collective-permute-start(bf16[2,192,768]{2,1,0:T(8,128)(2,1)S(1)} %get-tuple-element.62.oc_ref), channel_id=1, source_target_pairs={{0,16},{8,24},{1,17},{9,25},{2,18},{10,26},{3,19},{11,27},{4,20},{... | collective-permute-start | bytes 1769480 | tf_op jit(solution)/shard_map/ppermute | solution.py:527
  118.7 10.2 %collective-permute-start.50 = (bf16[192,768]{1,0:T(8,128)(2,1)S(1)}, bf16[192,768]{1,0:T(8,128)(2,1)S(1)}, u32[]{:S(2)}, u32[]{:S(2)}) collective-permute-start(bf16[192,768]{1,0:T(8,128)(2,1)S(1)} %dynamic-slice_convert_fusion.6), channel_id=1, source_target_pairs={{0,16},{8,24},{16,0},{24,8},{1,17},{9,25},{17,1},{25,9},{2,18},{10... | collective-permute-start | bytes 884744 | tf_op jit(solution)/shard_map/ppermute | solution.py:471
  130.1 9.4 %collective-permute-start.51 = (bf16[96,768]{1,0:T(8,128)(2,1)S(1)}, bf16[96,768]{1,0:T(8,128)(2,1)S(1)}, u32[]{:S(2)}, u32[]{:S(2)}) collective-permute-start(bf16[96,768]{1,0:T(8,128)(2,1)S(1)} %dynamic-slice_convert_fusion.12), channel_id=1, source_target_pairs={{0,1},{1,0},{2,3},{3,2},{4,5},{5,4},{6,7},{7,6},{8,9},{9,8},{10,11... | collective-permute-start | bytes 442376 | tf_op jit(solution)/shard_map/ppermute | solution.py:471
  141.2 28.8 %collective-permute-start.11 = (bf16[2,192,768]{2,1,0:T(8,128)(2,1)}, bf16[2,192,768]{2,1,0:T(8,128)(2,1)}, u32[]{:S(2)}, u32[]{:S(2)}) collective-permute-start(bf16[2,192,768]{2,1,0:T(8,128)(2,1)} %get-tuple-element.78), channel_id=1, source_target_pairs={{16,0},{24,8},{17,1},{25,9},{18,2},{26,10},{19,3},{27,11},{20,4},{... | collective-permute-start | bytes 1769480 | tf_op jit(solution)/shard_map/ppermute | solution.py:530
  142.5 28.5 %collective-permute-start.8 = (bf16[384,768]{1,0:T(8,128)(2,1)}, bf16[384,768]{1,0:T(8,128)(2,1)}, u32[]{:S(2)}, u32[]{:S(2)}) collective-permute-start(bf16[384,768]{1,0:T(8,128)(2,1)} %get-tuple-element.72), channel_id=1, source_target_pairs={{0,8},{8,0},{16,24},{24,16},{1,9},{9,1},{17,25},{25,17},{2,10},{10... | collective-permute-start | bytes 1769480 | tf_op jit(solution)/shard_map/ppermute | solution.py:471
  146.7 23.8 %collective-permute-start.9 = (bf16[192,768]{1,0:T(8,128)(2,1)}, bf16[192,768]{1,0:T(8,128)(2,1)}, u32[]{:S(2)}, u32[]{:S(2)}) collective-permute-start(bf16[192,768]{1,0:T(8,128)(2,1)} %get-tuple-element.76), channel_id=1, source_target_pairs={{16,0},{24,8},{17,1},{25,9},{18,2},{26,10},{19,3},{27,11},{20,4},{... | collective-permute-start | bytes 884744 | tf_op jit(solution)/shard_map/ppermute | solution.py:530
  147.9 23.0 %collective-permute-start.10 = (bf16[192,768]{1,0:T(8,128)(2,1)}, bf16[192,768]{1,0:T(8,128)(2,1)}, u32[]{:S(2)}, u32[]{:S(2)}) collective-permute-start(bf16[192,768]{1,0:T(8,128)(2,1)} %get-tuple-element.77), channel_id=1, source_target_pairs={{16,8},{24,0},{17,9},{25,1},{18,10},{26,2},{19,11},{27,3},{20,12},... | collective-permute-start | bytes 884744 | tf_op jit(solution)/shard_map/ppermute | solution.py:530
  154.2 15.8 %collective-permute-start.12 = (f32[3,2,768]{2,1,0:T(2,128)S(1)}, f32[3,2,768]{2,1,0:T(2,128)S(1)}, u32[]{:S(2)}, u32[]{:S(2)}) collective-permute-start(f32[3,2,768]{2,1,0:T(2,128)S(1)} %get-tuple-element.79), channel_id=1, source_target_pairs={{16,0},{24,8},{17,1},{25,9},{18,2},{26,10},{19,3},{27,11},{20,4},{... | collective-permute-start | bytes 55304 | tf_op jit(solution)/shard_map/ppermute | solution.py:530
  169.9 51.0 %collective-permute-start.15 = (bf16[768,768]{1,0:T(8,128)(2,1)S(1)}, bf16[768,768]{1,0:T(8,128)(2,1)S(1)}, u32[]{:S(2)}, u32[]{:S(2)}) collective-permute-start(bf16[768,768]{1,0:T(8,128)(2,1)S(1)} %get-tuple-element.52.normed_ref.n0_ref), channel_id=1, source_target_pairs={{0,8},{8,0},{16,24},{24,16},{1,9},{9,1},{17,25},{25,17},{2,10},{10... | collective-permute-start | bytes 3538952 | tf_op jit(solution)/shard_map/ppermute | solution.py:471
  170.0 103.7 %collective-permute-start.59 = (bf16[768,1536]{1,0:T(8,128)(2,1)}, bf16[768,1536]{1,0:T(8,128)(2,1)}, u32[]{:S(2)}, u32[]{:S(2)}) collective-permute-start(bf16[768,1536]{1,0:T(8,128)(2,1)} %get-tuple-element.92), channel_id=1, source_target_pairs={{0,8},{8,0},{16,24},{24,16},{1,9},{9,1},{17,25},{25,17},{2,10},{10... | collective-permute-start | bytes 7077896 | tf_op jit(solution)/shard_map/ppermute | solution.py:471
  170.5 22.7 %collective-permute-start.55 = (bf16[48,768]{1,0:T(8,128)(2,1)S(1)}, bf16[48,768]{1,0:T(8,128)(2,1)S(1)}, u32[]{:S(2)}, u32[]{:S(2)}) collective-permute-start(bf16[48,768]{1,0:T(8,128)(2,1)S(1)} %maximum_select_fusion.29), channel_id=1, source_target_pairs={{0,2},{1,3},{2,0},{3,1},{4,6},{5,7},{6,4},{7,5},{8,10},{9,11},{10,... | collective-permute-start | bytes 221192 | tf_op jit(solution)/shard_map/ppermute | solution.py:471
  190.4 33.3 %collective-permute-start.13 = (bf16[2,192,768]{2,1,0:T(8,128)(2,1)S(1)}, bf16[2,192,768]{2,1,0:T(8,128)(2,1)S(1)}, u32[]{:S(2)}, u32[]{:S(2)}) collective-permute-start(bf16[2,192,768]{2,1,0:T(8,128)(2,1)S(1)} %get-tuple-element.80), channel_id=1, source_target_pairs={{0,16},{8,24},{1,17},{9,25},{2,18},{10,26},{3,19},{11,27},{4,20},{... | collective-permute-start | bytes 1769480 | tf_op jit(solution)/shard_map/ppermute | solution.py:527
  191.9 31.8 %collective-permute-start.14 = (bf16[2,2,192,768]{3,2,1,0:T(8,128)(2,1)}, bf16[2,2,192,768]{3,2,1,0:T(8,128)(2,1)S(1)}, u32[]{:S(2)}, u32[]{:S(2)}) collective-permute-start(bf16[2,2,192,768]{3,2,1,0:T(8,128)(2,1)} %get-tuple-element.81.dkvc_ref), channel_id=1, source_target_pairs={{16,0},{24,8},{17,1},{25,9},{18,2},{26,10},{19,3},{27,11},{20,4},{... | collective-permute-start | bytes 3538952 | tf_op jit(solution)/shard_map/ppermute | solution.py:530
  193.3 27.6 %collective-permute-start.56 = (bf16[96,768]{1,0:T(8,128)(2,1)S(1)}, bf16[96,768]{1,0:T(8,128)(2,1)S(1)}, u32[]{:S(2)}, u32[]{:S(2)}) collective-permute-start(bf16[96,768]{1,0:T(8,128)(2,1)S(1)} %maximum_select_fusion.25), channel_id=1, source_target_pairs={{0,1},{1,0},{2,3},{3,2},{4,5},{5,4},{6,7},{7,6},{8,9},{9,8},{10,11... | collective-permute-start | bytes 442376 | tf_op jit(solution)/shard_map/ppermute | solution.py:471
  220.9 62.8 %collective-permute-start.69 = (bf16[1536,768]{1,0:T(8,128)(2,1)S(1)}, bf16[1536,768]{1,0:T(8,128)(2,1)S(1)}, u32[]{:S(2)}, u32[]{:S(2)}) collective-permute-start(bf16[1536,768]{1,0:T(8,128)(2,1)S(1)} %copy-done.35), channel_id=1, source_target_pairs={{0,8},{8,0},{16,24},{24,16},{1,9},{9,1},{17,25},{25,17},{2,10},{10... | collective-permute-start | bytes 7077896 | tf_op jit(solution)/shard_map/ppermute | solution.py:471
  221.0 14.8 %collective-permute-start.57 = (bf16[192,768]{1,0:T(8,128)(2,1)S(1)}, bf16[192,768]{1,0:T(8,128)(2,1)S(1)}, u32[]{:S(2)}, u32[]{:S(2)}) collective-permute-start(bf16[192,768]{1,0:T(8,128)(2,1)S(1)} %maximum_select_fusion.19), channel_id=1, source_target_pairs={{0,16},{8,24},{16,0},{24,8},{1,17},{9,25},{17,1},{25,9},{2,18},{10... | collective-permute-start | bytes 884744 | tf_op jit(solution)/shard_map/ppermute | solution.py:471
  234.1 9.2 %collective-permute-start.31 = (bf16[384,384]{1,0:T(8,128)(2,1)S(1)}, bf16[384,384]{1,0:T(8,128)(2,1)S(1)}, u32[]{:S(2)}, u32[]{:S(2)}) collective-permute-start(bf16[384,384]{1,0:T(8,128)(2,1)S(1)} %fusion.4), channel_id=1, source_target_pairs={{0,2},{1,3},{2,0},{3,1},{4,6},{5,7},{6,4},{7,5},{8,10},{9,11},{10,... | collective-permute-start | bytes 884744 | tf_op jit(solution)/shard_map/ppermute | solution.py:471
  236.0 198.8 %collective-permute-start.16 = (bf16[1152,768]{1,0:T(8,128)(2,1)S(1)}, bf16[1152,768]{1,0:T(8,128)(2,1)S(1)}, u32[]{:S(2)}, u32[]{:S(2)}) collective-permute-start(bf16[1152,768]{1,0:T(8,128)(2,1)S(1)} %copy-done.36), channel_id=1, source_target_pairs={{0,8},{8,0},{16,24},{24,16},{1,9},{9,1},{17,25},{25,17},{2,10},{10... | collective-permute-start | bytes 5308424 | tf_op jit(solution)/shard_map/ppermute | solution.py:471
  236.1 16.1 %collective-permute-start.40 = (bf16[384,384]{1,0:T(8,128)(2,1)S(1)}, bf16[384,384]{1,0:T(8,128)(2,1)S(1)}, u32[]{:S(2)}, u32[]{:S(2)}) collective-permute-start(bf16[384,384]{1,0:T(8,128)(2,1)S(1)} %fusion.5), channel_id=1, source_target_pairs={{0,16},{8,24},{16,0},{24,8},{1,17},{9,25},{17,1},{25,9},{2,18},{10... | collective-permute-start | bytes 884744 | tf_op jit(solution)/shard_map/ppermute | solution.py:471
  243.3 14.8 %collective-permute-start.22 = (bf16[384,384]{1,0:T(8,128)(2,1)S(1)}, bf16[384,384]{1,0:T(8,128)(2,1)S(1)}, u32[]{:S(2)}, u32[]{:S(2)}) collective-permute-start(bf16[384,384]{1,0:T(8,128)(2,1)S(1)} %fusion.3), channel_id=1, source_target_pairs={{0,1},{1,0},{2,3},{3,2},{4,5},{5,4},{6,7},{7,6},{8,9},{9,8},{10,11... | collective-permute-start | bytes 884744 | tf_op jit(solution)/shard_map/ppermute | solution.py:471
  252.2 11.4 %collective-permute-start.32 = (bf16[192,384]{1,0:T(8,128)(2,1)S(1)}, bf16[192,384]{1,0:T(8,128)(2,1)S(1)}, u32[]{:S(2)}, u32[]{:S(2)}) collective-permute-start(bf16[192,384]{1,0:T(8,128)(2,1)S(1)} %dynamic-slice_convert_fusion.14), channel_id=1, source_target_pairs={{0,4},{1,5},{2,6},{3,7},{4,0},{5,1},{6,2},{7,3},{8,12},{9,13},{10,... | collective-permute-start | bytes 442376 | tf_op jit(solution)/shard_map/ppermute | solution.py:471
  258.1 5.9 %collective-permute-start.41 = (bf16[192,384]{1,0:T(8,128)(2,1)S(1)}, bf16[192,384]{1,0:T(8,128)(2,1)S(1)}, u32[]{:S(2)}, u32[]{:S(2)}) collective-permute-start(bf16[192,384]{1,0:T(8,128)(2,1)S(1)} %dynamic-slice_convert_fusion.13), channel_id=1, source_target_pairs={{0,1},{1,0},{2,3},{3,2},{4,5},{5,4},{6,7},{7,6},{8,9},{9,8},{10,11... | collective-permute-start | bytes 442376 | tf_op jit(solution)/shard_map/ppermute | solution.py:471
  269.4 10.6 %collective-permute-start.24 = (bf16[96,384]{1,0:T(8,128)(2,1)S(1)}, bf16[96,384]{1,0:T(8,128)(2,1)S(1)}, u32[]{:S(2)}, u32[]{:S(2)}) collective-permute-start(bf16[96,384]{1,0:T(8,128)(2,1)S(1)} %dynamic-slice_convert_fusion.19), channel_id=1, source_target_pairs={{0,2},{1,3},{2,0},{3,1},{4,6},{5,7},{6,4},{7,5},{8,10},{9,11},{10,... | collective-permute-start | bytes 221192 | tf_op jit(solution)/shard_map/ppermute | solution.py:471
  273.2 8.5 %collective-permute-start.34 = (bf16[48,384]{1,0:T(8,128)(2,1)S(1)}, bf16[48,384]{1,0:T(8,128)(2,1)S(1)}, u32[]{:S(2)}, u32[]{:S(2)}) collective-permute-start(bf16[48,384]{1,0:T(8,128)(2,1)S(1)} %dynamic-slice_convert_fusion.22), channel_id=1, source_target_pairs={{0,16},{8,24},{16,0},{24,8},{1,17},{9,25},{17,1},{25,9},{2,18},{10... | collective-permute-start | bytes 110600 | tf_op jit(solution)/shard_map/ppermute | solution.py:471
  273.6 8.2 %collective-permute-start.43 = (bf16[48,384]{1,0:T(8,128)(2,1)S(1)}, bf16[48,384]{1,0:T(8,128)(2,1)S(1)}, u32[]{:S(2)}, u32[]{:S(2)}) collective-permute-start(bf16[48,384]{1,0:T(8,128)(2,1)S(1)} %dynamic-slice_convert_fusion.21), channel_id=1, source_target_pairs={{0,4},{1,5},{2,6},{3,7},{4,0},{5,1},{6,2},{7,3},{8,12},{9,13},{10,... | collective-permute-start | bytes 110600 | tf_op jit(solution)/shard_map/ppermute | solution.py:471
  280.0 26.4 %collective-permute-start.60 = (bf16[384,1536]{1,0:T(8,128)(2,1)S(1)}, bf16[384,1536]{1,0:T(8,128)(2,1)S(1)}, u32[]{:S(2)}, u32[]{:S(2)}) collective-permute-start(bf16[384,1536]{1,0:T(8,128)(2,1)S(1)} %dynamic-slice_convert_fusion.1), channel_id=1, source_target_pairs={{0,2},{1,3},{2,0},{3,1},{4,6},{5,7},{6,4},{7,5},{8,10},{9,11},{10,... | collective-permute-start | bytes 3538952 | tf_op jit(solution)/shard_map/ppermute | solution.py:471
  281.7 25.4 %collective-permute-start.25 = (bf16[48,384]{1,0:T(8,128)(2,1)S(1)}, bf16[48,384]{1,0:T(8,128)(2,1)S(1)}, u32[]{:S(2)}, u32[]{:S(2)}) collective-permute-start(bf16[48,384]{1,0:T(8,128)(2,1)S(1)} %dynamic-slice_convert_fusion.23), channel_id=1, source_target_pairs={{0,4},{1,5},{2,6},{3,7},{4,0},{5,1},{6,2},{7,3},{8,12},{9,13},{10,... | collective-permute-start | bytes 110600 | tf_op jit(solution)/shard_map/ppermute | solution.py:471
  281.8 26.0 %collective-permute-start.35 = (bf16[48,384]{1,0:T(8,128)(2,1)S(1)}, bf16[48,384]{1,0:T(8,128)(2,1)S(1)}, u32[]{:S(2)}, u32[]{:S(2)}) collective-permute-start(bf16[48,384]{1,0:T(8,128)(2,1)S(1)} %add_convert_fusion.4), channel_id=1, source_target_pairs={{0,16},{8,24},{16,0},{24,8},{1,17},{9,25},{17,1},{25,9},{2,18},{10... | collective-permute-start | bytes 110600 | tf_op jit(solution)/shard_map/ppermute | solution.py:471
  283.7 27.1 %collective-permute-start.44 = (bf16[48,384]{1,0:T(8,128)(2,1)S(1)}, bf16[48,384]{1,0:T(8,128)(2,1)S(1)}, u32[]{:S(2)}, u32[]{:S(2)}) collective-permute-start(bf16[48,384]{1,0:T(8,128)(2,1)S(1)} %add_convert_fusion.3), channel_id=1, source_target_pairs={{0,4},{1,5},{2,6},{3,7},{4,0},{5,1},{6,2},{7,3},{8,12},{9,13},{10,... | collective-permute-start | bytes 110600 | tf_op jit(solution)/shard_map/ppermute | solution.py:471
  306.9 27.0 %collective-permute-start.61 = (bf16[192,1536]{1,0:T(8,128)(2,1)S(1)}, bf16[192,1536]{1,0:T(8,128)(2,1)S(1)}, u32[]{:S(2)}, u32[]{:S(2)}) collective-permute-start(bf16[192,1536]{1,0:T(8,128)(2,1)S(1)} %dynamic-slice_convert_fusion.3), channel_id=1, source_target_pairs={{0,4},{1,5},{2,6},{3,7},{4,0},{5,1},{6,2},{7,3},{8,12},{9,13},{10,... | collective-permute-start | bytes 1769480 | tf_op jit(solution)/shard_map/ppermute | solution.py:471
  307.1 28.9 %collective-permute-start.70 = (bf16[768,768]{1,0:T(8,128)(2,1)S(1)}, bf16[768,768]{1,0:T(8,128)(2,1)S(1)}, u32[]{:S(2)}, u32[]{:S(2)}) collective-permute-start(bf16[768,768]{1,0:T(8,128)(2,1)S(1)} %dynamic-slice_convert_fusion), channel_id=1, source_target_pairs={{0,1},{1,0},{2,3},{3,2},{4,5},{5,4},{6,7},{7,6},{8,9},{9,8},{10,11... | collective-permute-start | bytes 3538952 | tf_op jit(solution)/shard_map/ppermute | solution.py:471
  307.8 25.8 %collective-permute-start.26 = (bf16[48,384]{1,0:T(8,128)(2,1)S(1)}, bf16[48,384]{1,0:T(8,128)(2,1)S(1)}, u32[]{:S(2)}, u32[]{:S(2)}) collective-permute-start(bf16[48,384]{1,0:T(8,128)(2,1)S(1)} %add_convert_fusion.5), channel_id=1, source_target_pairs={{0,4},{1,5},{2,6},{3,7},{4,0},{5,1},{6,2},{7,3},{8,12},{9,13},{10,... | collective-permute-start | bytes 110600 | tf_op jit(solution)/shard_map/ppermute | solution.py:471
  310.8 90.1 %collective-permute-start.36 = (bf16[96,384]{1,0:T(8,128)(2,1)S(1)}, bf16[96,384]{1,0:T(8,128)(2,1)S(1)}, u32[]{:S(2)}, u32[]{:S(2)}) collective-permute-start(bf16[96,384]{1,0:T(8,128)(2,1)S(1)} %maximum_select_fusion.27), channel_id=1, source_target_pairs={{0,1},{1,0},{2,3},{3,2},{4,5},{5,4},{6,7},{7,6},{8,9},{9,8},{10,11... | collective-permute-start | bytes 221192 | tf_op jit(solution)/shard_map/ppermute | solution.py:471
  333.6 43.5 %collective-permute-start.45 = (bf16[96,384]{1,0:T(8,128)(2,1)S(1)}, bf16[96,384]{1,0:T(8,128)(2,1)S(1)}, u32[]{:S(2)}, u32[]{:S(2)}) collective-permute-start(bf16[96,384]{1,0:T(8,128)(2,1)S(1)} %maximum_select_fusion.28), channel_id=1, source_target_pairs={{0,2},{1,3},{2,0},{3,1},{4,6},{5,7},{6,4},{7,5},{8,10},{9,11},{10,... | collective-permute-start | bytes 221192 | tf_op jit(solution)/shard_map/ppermute | solution.py:471
  333.9 68.5 %collective-permute-start.27 = (bf16[96,384]{1,0:T(8,128)(2,1)S(1)}, bf16[96,384]{1,0:T(8,128)(2,1)S(1)}, u32[]{:S(2)}, u32[]{:S(2)}) collective-permute-start(bf16[96,384]{1,0:T(8,128)(2,1)S(1)} %maximum_select_fusion.26), channel_id=1, source_target_pairs={{0,2},{1,3},{2,0},{3,1},{4,6},{5,7},{6,4},{7,5},{8,10},{9,11},{10,... | collective-permute-start | bytes 221192 | tf_op jit(solution)/shard_map/ppermute | solution.py:471
  336.0 8.3 %collective-permute-start.62 = (bf16[96,1536]{1,0:T(8,128)(2,1)S(1)}, bf16[96,1536]{1,0:T(8,128)(2,1)S(1)}, u32[]{:S(2)}, u32[]{:S(2)}) collective-permute-start(bf16[96,1536]{1,0:T(8,128)(2,1)S(1)} %dynamic-slice_convert_fusion.5), channel_id=1, source_target_pairs={{0,1},{1,0},{2,3},{3,2},{4,5},{5,4},{6,7},{7,6},{8,9},{9,8},{10,11... | collective-permute-start | bytes 884744 | tf_op jit(solution)/shard_map/ppermute | solution.py:471
  344.3 13.9 %collective-permute-start.71 = (bf16[384,768]{1,0:T(8,128)(2,1)S(1)}, bf16[384,768]{1,0:T(8,128)(2,1)S(1)}, u32[]{:S(2)}, u32[]{:S(2)}) collective-permute-start(bf16[384,768]{1,0:T(8,128)(2,1)S(1)} %dynamic-slice_convert_fusion.2), channel_id=1, source_target_pairs={{0,16},{8,24},{16,0},{24,8},{1,17},{9,25},{17,1},{25,9},{2,18},{10... | collective-permute-start | bytes 1769480 | tf_op jit(solution)/shard_map/ppermute | solution.py:471
  363.3 6.7 %collective-permute-start.72 = (bf16[192,768]{1,0:T(8,128)(2,1)S(1)}, bf16[192,768]{1,0:T(8,128)(2,1)S(1)}, u32[]{:S(2)}, u32[]{:S(2)}) collective-permute-start(bf16[192,768]{1,0:T(8,128)(2,1)S(1)} %dynamic-slice_convert_fusion.4), channel_id=1, source_target_pairs={{0,2},{1,3},{2,0},{3,1},{4,6},{5,7},{6,4},{7,5},{8,10},{9,11},{10,... | collective-permute-start | bytes 884744 | tf_op jit(solution)/shard_map/ppermute | solution.py:471
  375.2 10.6 %collective-permute-start.73 = (bf16[96,768]{1,0:T(8,128)(2,1)S(1)}, bf16[96,768]{1,0:T(8,128)(2,1)S(1)}, u32[]{:S(2)}, u32[]{:S(2)}) collective-permute-start(bf16[96,768]{1,0:T(8,128)(2,1)S(1)} %dynamic-slice_convert_fusion.10), channel_id=1, source_target_pairs={{0,4},{1,5},{2,6},{3,7},{4,0},{5,1},{6,2},{7,3},{8,12},{9,13},{10,... | collective-permute-start | bytes 442376 | tf_op jit(solution)/shard_map/ppermute | solution.py:471
  377.2 9.3 %collective-permute-start.65 = (bf16[96,1536]{1,0:T(8,128)(2,1)S(1)}, bf16[96,1536]{1,0:T(8,128)(2,1)S(1)}, u32[]{:S(2)}, u32[]{:S(2)}) collective-permute-start(bf16[96,1536]{1,0:T(8,128)(2,1)S(1)} %maximum_select_fusion.20), channel_id=1, source_target_pairs={{0,1},{1,0},{2,3},{3,2},{4,5},{5,4},{6,7},{7,6},{8,9},{9,8},{10,11... | collective-permute-start | bytes 884744 | tf_op jit(solution)/shard_map/ppermute | solution.py:471
  385.8 18.2 %collective-permute-start.46 = (bf16[192,384]{1,0:T(8,128)(2,1)S(1)}, bf16[192,384]{1,0:T(8,128)(2,1)S(1)}, u32[]{:S(2)}, u32[]{:S(2)}) collective-permute-start(bf16[192,384]{1,0:T(8,128)(2,1)S(1)} %maximum_select_fusion.24), channel_id=1, source_target_pairs={{0,1},{1,0},{2,3},{3,2},{4,5},{5,4},{6,7},{7,6},{8,9},{9,8},{10,11... | collective-permute-start | bytes 442376 | tf_op jit(solution)/shard_map/ppermute | solution.py:471
  386.5 14.3 %collective-permute-start.74 = (bf16[96,768]{1,0:T(8,128)(2,1)S(1)}, bf16[96,768]{1,0:T(8,128)(2,1)S(1)}, u32[]{:S(2)}, u32[]{:S(2)}) collective-permute-start(bf16[96,768]{1,0:T(8,128)(2,1)S(1)} %add_convert_fusion), channel_id=1, source_target_pairs={{0,4},{1,5},{2,6},{3,7},{4,0},{5,1},{6,2},{7,3},{8,12},{9,13},{10,... | collective-permute-start | bytes 442376 | tf_op jit(solution)/shard_map/ppermute | solution.py:471
  400.8 21.8 %collective-permute-start.66 = (bf16[192,1536]{1,0:T(8,128)(2,1)S(1)}, bf16[192,1536]{1,0:T(8,128)(2,1)S(1)}, u32[]{:S(2)}, u32[]{:S(2)}) collective-permute-start(bf16[192,1536]{1,0:T(8,128)(2,1)S(1)} %maximum_select_fusion.14), channel_id=1, source_target_pairs={{0,4},{1,5},{2,6},{3,7},{4,0},{5,1},{6,2},{7,3},{8,12},{9,13},{10,... | collective-permute-start | bytes 1769480 | tf_op jit(solution)/shard_map/ppermute | solution.py:471
  400.8 10.5 %collective-permute-start.75 = (bf16[192,768]{1,0:T(8,128)(2,1)S(1)}, bf16[192,768]{1,0:T(8,128)(2,1)S(1)}, u32[]{:S(2)}, u32[]{:S(2)}) collective-permute-start(bf16[192,768]{1,0:T(8,128)(2,1)S(1)} %maximum_select_fusion.21), channel_id=1, source_target_pairs={{0,2},{1,3},{2,0},{3,1},{4,6},{5,7},{6,4},{7,5},{8,10},{9,11},{10,... | collective-permute-start | bytes 884744 | tf_op jit(solution)/shard_map/ppermute | solution.py:471
  402.5 22.5 %collective-permute-start.37 = (bf16[192,384]{1,0:T(8,128)(2,1)S(1)}, bf16[192,384]{1,0:T(8,128)(2,1)S(1)}, u32[]{:S(2)}, u32[]{:S(2)}) collective-permute-start(bf16[192,384]{1,0:T(8,128)(2,1)S(1)} %maximum_select_fusion.23), channel_id=1, source_target_pairs={{0,4},{1,5},{2,6},{3,7},{4,0},{5,1},{6,2},{7,3},{8,12},{9,13},{10,... | collective-permute-start | bytes 442376 | tf_op jit(solution)/shard_map/ppermute | solution.py:471
  404.0 20.8 %collective-permute-start.28 = (bf16[192,384]{1,0:T(8,128)(2,1)S(1)}, bf16[192,384]{1,0:T(8,128)(2,1)S(1)}, u32[]{:S(2)}, u32[]{:S(2)}) collective-permute-start(bf16[192,384]{1,0:T(8,128)(2,1)S(1)} %maximum_select_fusion.22), channel_id=1, source_target_pairs={{0,16},{8,24},{16,0},{24,8},{1,17},{9,25},{17,1},{25,9},{2,18},{10... | collective-permute-start | bytes 442376 | tf_op jit(solution)/shard_map/ppermute | solution.py:471
  411.4 14.4 %collective-permute-start.47 = (bf16[384,384]{1,0:T(8,128)(2,1)S(1)}, bf16[384,384]{1,0:T(8,128)(2,1)S(1)}, u32[]{:S(2)}, u32[]{:S(2)}) collective-permute-start(bf16[384,384]{1,0:T(8,128)(2,1)S(1)} %maximum_select_fusion.18), channel_id=1, source_target_pairs={{0,16},{8,24},{16,0},{24,8},{1,17},{9,25},{17,1},{25,9},{2,18},{10... | collective-permute-start | bytes 884744 | tf_op jit(solution)/shard_map/ppermute | solution.py:471
  422.6 10.8 %collective-permute-start.76 = (bf16[384,768]{1,0:T(8,128)(2,1)S(1)}, bf16[384,768]{1,0:T(8,128)(2,1)S(1)}, u32[]{:S(2)}, u32[]{:S(2)}) collective-permute-start(bf16[384,768]{1,0:T(8,128)(2,1)S(1)} %maximum_select_fusion.15), channel_id=1, source_target_pairs={{0,16},{8,24},{16,0},{24,8},{1,17},{9,25},{17,1},{25,9},{2,18},{10... | collective-permute-start | bytes 1769480 | tf_op jit(solution)/shard_map/ppermute | solution.py:471
  424.8 27.7 %collective-permute-start.67 = (bf16[384,1536]{1,0:T(8,128)(2,1)S(1)}, bf16[384,1536]{1,0:T(8,128)(2,1)S(1)}, u32[]{:S(2)}, u32[]{:S(2)}) collective-permute-start(bf16[384,1536]{1,0:T(8,128)(2,1)S(1)} %maximum_select_fusion.8), channel_id=1, source_target_pairs={{0,2},{1,3},{2,0},{3,1},{4,6},{5,7},{6,4},{7,5},{8,10},{9,11},{10,... | collective-permute-start | bytes 3538952 | tf_op jit(solution)/shard_map/ppermute | solution.py:471
  425.0 8.8 %collective-permute-start.29 = (bf16[384,384]{1,0:T(8,128)(2,1)S(1)}, bf16[384,384]{1,0:T(8,128)(2,1)S(1)}, u32[]{:S(2)}, u32[]{:S(2)}) collective-permute-start(bf16[384,384]{1,0:T(8,128)(2,1)S(1)} %maximum_select_fusion.16), channel_id=1, source_target_pairs={{0,1},{1,0},{2,3},{3,2},{4,5},{5,4},{6,7},{7,6},{8,9},{9,8},{10,11... | collective-permute-start | bytes 884744 | tf_op jit(solution)/shard_map/ppermute | solution.py:471
  425.8 32.6 %collective-permute-start.58 = (bf16[384,768]{1,0:T(8,128)(2,1)S(1)}, bf16[384,768]{1,0:T(8,128)(2,1)S(1)}, u32[]{:S(2)}, u32[]{:S(2)}) collective-permute-start(bf16[384,768]{1,0:T(8,128)(2,1)S(1)} %maximum_select_fusion.13), channel_id=1, source_target_pairs={{0,8},{8,0},{16,24},{24,16},{1,9},{9,1},{17,25},{25,17},{2,10},{10... | collective-permute-start | bytes 1769480 | tf_op jit(solution)/shard_map/ppermute | solution.py:471
  433.3 25.6 %collective-permute-start.38 = (bf16[384,384]{1,0:T(8,128)(2,1)S(1)}, bf16[384,384]{1,0:T(8,128)(2,1)S(1)}, u32[]{:S(2)}, u32[]{:S(2)}) collective-permute-start(bf16[384,384]{1,0:T(8,128)(2,1)S(1)} %maximum_select_fusion.17), channel_id=1, source_target_pairs={{0,2},{1,3},{2,0},{3,1},{4,6},{5,7},{6,4},{7,5},{8,10},{9,11},{10,... | collective-permute-start | bytes 884744 | tf_op jit(solution)/shard_map/ppermute | solution.py:471
  433.8 23.7 %collective-permute-start.77 = (bf16[768,768]{1,0:T(8,128)(2,1)S(1)}, bf16[768,768]{1,0:T(8,128)(2,1)S(1)}, u32[]{:S(2)}, u32[]{:S(2)}) collective-permute-start(bf16[768,768]{1,0:T(8,128)(2,1)S(1)} %maximum_select_fusion.9), channel_id=1, source_target_pairs={{0,1},{1,0},{2,3},{3,2},{4,5},{5,4},{6,7},{7,6},{8,9},{9,8},{10,11... | collective-permute-start | bytes 3538952 | tf_op jit(solution)/shard_map/ppermute | solution.py:471
  434.8 30.7 %collective-permute-start.30 = (bf16[768,384]{1,0:T(8,128)(2,1)S(1)}, bf16[768,384]{1,0:T(8,128)(2,1)S(1)}, u32[]{:S(2)}, u32[]{:S(2)}) collective-permute-start(bf16[768,384]{1,0:T(8,128)(2,1)S(1)} %maximum_select_fusion.10), channel_id=1, source_target_pairs={{0,8},{8,0},{16,24},{24,16},{1,9},{9,1},{17,25},{25,17},{2,10},{10... | collective-permute-start | bytes 1769480 | tf_op jit(solution)/shard_map/ppermute | solution.py:471
  453.3 29.8 %collective-permute-start.68 = (bf16[768,1536]{1,0:T(8,128)(2,1)S(1)}, bf16[768,1536]{1,0:T(8,128)(2,1)S(1)}, u32[]{:S(2)}, u32[]{:S(2)}) collective-permute-start(bf16[768,1536]{1,0:T(8,128)(2,1)S(1)} %maximum_select_fusion.2), channel_id=1, source_target_pairs={{0,8},{8,0},{16,24},{24,16},{1,9},{9,1},{17,25},{25,17},{2,10},{10... | collective-permute-start | bytes 7077896 | tf_op jit(solution)/shard_map/ppermute | solution.py:471
  458.2 29.2 %collective-permute-start.78 = (bf16[1536,768]{1,0:T(8,128)(2,1)S(1)}, bf16[1536,768]{1,0:T(8,128)(2,1)S(1)}, u32[]{:S(2)}, u32[]{:S(2)}) collective-permute-start(bf16[1536,768]{1,0:T(8,128)(2,1)S(1)} %maximum_select_fusion.3), channel_id=1, source_target_pairs={{0,8},{8,0},{16,24},{24,16},{1,9},{9,1},{17,25},{25,17},{2,10},{10... | collective-permute-start | bytes 7077896 | tf_op jit(solution)/shard_map/ppermute | solution.py:471
  458.4 11.7 %collective-permute-start.48 = (bf16[768,384]{1,0:T(8,128)(2,1)S(1)}, bf16[768,384]{1,0:T(8,128)(2,1)S(1)}, u32[]{:S(2)}, u32[]{:S(2)}) collective-permute-start(bf16[768,384]{1,0:T(8,128)(2,1)S(1)} %maximum_select_fusion.12), channel_id=1, source_target_pairs={{0,8},{8,0},{16,24},{24,16},{1,9},{9,1},{17,25},{25,17},{2,10},{10... | collective-permute-start | bytes 1769480 | tf_op jit(solution)/shard_map/ppermute | solution.py:471
  463.7 11.1 %collective-permute-start.39 = (bf16[768,384]{1,0:T(8,128)(2,1)S(1)}, bf16[768,384]{1,0:T(8,128)(2,1)S(1)}, u32[]{:S(2)}, u32[]{:S(2)}) collective-permute-start(bf16[768,384]{1,0:T(8,128)(2,1)S(1)} %maximum_select_fusion.11), channel_id=1, source_target_pairs={{0,8},{8,0},{16,24},{24,16},{1,9},{9,1},{17,25},{25,17},{2,10},{10... | collective-permute-start | bytes 1769480 | tf_op jit(solution)/shard_map/ppermute | solution.py:471
  (57 other events, 591.1 us)
